TPU v7x, 32 devices: a whole 2x2x4 slice. The times are simulated.
32 devices in a mesh: section: 4 (over y, core), dp: 4 (over z), expert: 2 (over x).
Axes of the slice: x: 2, y: 2, z: 4, core: 2. Of those that a mesh axis runs over, the one named last changes fastest.
Arguments:
- stream: bfloat16 [4, 1024, 2048], P('section', ('dp', 'expert')), may hold values from -60 to 60
- norm_gain: bfloat16 [4, 2048], P('section'), may hold values from 0.29882812 to 3
- gate_probs: float32 [4, 1024, 8], P('section', ('dp', 'expert')), may hold values from 0.02 to 1
- expert_ids: int32 [4, 1024, 8], P('section', ('dp', 'expert')), may hold values from 0 to 127, as said below
- gate_up_weight: bfloat16 [4, 2, 2, 2048, 1024], P('section', 'expert', None, None, 'dp'), may hold values from -0.125 to 0.125
- down_weight: bfloat16 [4, 2, 1024, 2048], P('section', 'expert', 'dp'), may hold values from -0.1875 to 0.1875
Outputs:
- handed: bfloat16 [4, 1024, 2048], P('section', ('dp', 'expert'))
Inputs may be any that keep to these rules, and one draw needn't show every extreme that they name: `expert_ids`: each row names 8 different experts. In the rows of one device each expert below 2 is named by at most 12 rows; in each section one such expert is named by exactly 12 rows in the rows of every device.
All inputs are finite; a program needn't handle non-finite values.
Results may differ from a plain program's by a relative error of at most 0.0077.
Values may be sent and summed in bfloat16 or wider, within the bound.
No kernel may reach another device: no remote copies, remote signals or barrier semaphores. Data moves between devices by JAX's collectives and lax.ppermute only.
A program may use at most 128 MiB of HBM per device.

v0:
```python
import jax
import jax.numpy as jnp
from jax import lax
from jax.sharding import PartitionSpec as P

CAP = 12


epsilon = 1e-06


def from_behind(value, axis, steps):
    count = lax.axis_size(axis)
    pairs = [(source, (source + steps) % count) for source in range(count)]
    return lax.ppermute(value, axis, pairs)


def normalize(activations, gain_row):
    widened = activations.astype(jnp.float32)
    inverse_rms = lax.rsqrt(jnp.mean(widened * widened, axis=-1, keepdims=True) + epsilon)
    return (widened * inverse_rms * gain_row.astype(jnp.float32)).astype(jnp.bfloat16)


def slot_tables(gate_probs, expert_ids, held_count, capacity):
    weights = gate_probs / jnp.sum(gate_probs, axis=-1, keepdims=True)
    experts = jnp.arange(held_count, dtype=jnp.int32)
    matches = expert_ids[..., None] == experts
    coefficient = jnp.sum(jnp.where(matches, weights[..., None], jnp.float32(0.0)), axis=-2)
    chosen = jnp.any(matches, axis=-2).astype(jnp.int32)
    position = jnp.cumsum(chosen, axis=-2) - chosen
    places = jnp.arange(capacity, dtype=jnp.int32)
    slot_table = (chosen[..., None] == 1) & (position[..., None] == places)
    return (coefficient, slot_table)


def expert_quarter(slot_rows, gate_up, down_matrix):
    gate_rows = jnp.dot(slot_rows, gate_up[0], preferred_element_type=jnp.float32)
    up_rows = jnp.dot(slot_rows, gate_up[1], preferred_element_type=jnp.float32)
    hidden = (jax.nn.silu(gate_rows) * up_rows).astype(jnp.bfloat16)
    return jnp.dot(hidden, down_matrix, preferred_element_type=jnp.float32).astype(jnp.bfloat16)


def shards(stream, norm_gain, gate_probs, expert_ids, gate_up_weight, down_weight):
    normed = normalize(stream[0], norm_gain[0])
    held_count = lax.axis_size("expert")
    group_count = lax.axis_size("dp")
    coefficient, slot_table = slot_tables(gate_probs[0], expert_ids[0], held_count, CAP)
    slot_onehot = slot_table.astype(jnp.bfloat16)
    packed = jnp.einsum(
        "tec,td->ecd", slot_onehot, normed, preferred_element_type=jnp.float32
    ).astype(jnp.bfloat16)
    gate_up = gate_up_weight[0, 0]
    down_matrix = down_weight[0, 0]
    feature_count = normed.shape[1]
    capacity = packed.shape[1]
    fanned = jnp.broadcast_to(packed[None], (group_count,) + packed.shape)
    fanned = fanned.reshape(group_count * held_count, capacity, feature_count)
    received = lax.all_to_all(fanned, ("dp", "expert"), split_axis=0, concat_axis=0, tiled=True)
    slot_count = received.shape[1]
    partial_rows = expert_quarter(received.reshape(-1, feature_count), gate_up, down_matrix)
    partial_rows = partial_rows.reshape(group_count * held_count, slot_count, feature_count)
    returned = lax.all_to_all(
        partial_rows, ("dp", "expert"), split_axis=0, concat_axis=0, tiled=True
    )
    returned = returned.reshape(group_count, held_count, capacity, feature_count)
    rounded = jnp.sum(returned.astype(jnp.float32), axis=0).astype(jnp.bfloat16)
    expert_sums = lax.optimization_barrier(rounded).astype(jnp.float32)
    shares = slot_table.astype(jnp.float32) * coefficient[..., None]
    mixture = jnp.einsum(
        "tec,ecd->td", shares, expert_sums, precision=lax.Precision.HIGHEST
    ).astype(jnp.bfloat16)
    return from_behind(mixture[None], "section", 1)


def solution(mesh):
    in_specs = (
        P("section", ("dp", "expert"), None),
        P("section", None),
        P("section", ("dp", "expert"), None),
        P("section", ("dp", "expert"), None),
        P("section", "expert", None, None, "dp"),
        P("section", "expert", "dp", None),
    )
    out_specs = P("section", ("dp", "expert"), None)
    return jax.shard_map(shards, mesh=mesh, in_specs=in_specs, out_specs=out_specs, check_vma=False)
```

profile of v0, /device:TPU:0, one launch (start us, length us, event | category | flops | bytes accessed | tf_op | source)
XLA Modules:
  0.0 58.6 jit_solution(12711369605780565142)
XLA Ops:
  0.0 0.0 copy-start
  0.0 0.8 %fusion.33 = pred[128,2]{0,1:T(4,128)(4,1)S(1)} fusion(s32[128,8]{0,1:T(8,128)} %bitcast.39), kind=kLoop, calls=%fused_computation.37 | loop fusion | flops 3840 | bytes 4352 | tf_op jit(solution)/shard_map/reduce_or | solution.py:29
  0.8 0.1 copy.19
  0.9 0.2 reduce_window_sum.11
  1.1 0.1 copy.20
  1.2 0.7 %mul.50 = f32[1,2048]{1,0:T(1,128)S(1)} convert(bf16[1,2048]{1,0:T(2,128)(2,1)} %param.7) | non-fusion elementwise | flops 2048 | bytes 12288 | tf_op jit(solution)/shard_map/mul | solution.py:21
  1.9 1.2 %fusion.3 = f32[128]{0:T(128)S(1)} fusion(bf16[1,128,2048]{2,1,0:T(8,128)(2,1)} %param.6), kind=kLoop, calls=%fused_computation.9 | loop fusion | flops 786304 | bytes 524800 | tf_op jit(solution)/shard_map/reduce_sum | solution.py:20
  3.1 1.4 %convolution_convert_fusion.1 = bf16[2,12,2048]{2,1,0:T(8,128)(2,1)S(1)} fusion(bf16[1,128,2048]{2,1,0:T(8,128)(2,1)} %param.6, f32[2048]{0:T(1024)S(1)} %bitcast.41, f32[128]{0:T(128)S(1)} %add_rsqrt_fusion, s32[128,2]{0,1:T(2,128)S(1)} %convert_subtract_fusion, pred[128,2]{0,1:T(4,128)(4,1)S(1)} %get-tuple-element.5), kind=kOutput, calls=%fused_computation.4 | convolution fusion | flops 13686784 | bytes 632576 | tf_op jit(solution)/shard_map/tec,td->ecd/dot_general | solution.py:49
  4.5 21.6 %all_to_all.10 = bf16[8,12,2048]{2,1,0:T(8,128)(2,1)S(1)} all-to-all(bf16[8,12,2048]{2,1,0:T(8,128)(2,1)S(1)} %bitcast.37), channel_id=1, replica_groups=mesh['section'=4,'dp'=4,'expert'=2] {'dp','expert'}, dimensions={0} | all-to-all | bytes 786432 | tf_op jit(solution)/shard_map/all_to_all | solution.py:58
  26.1 0.1 reshape.66
  26.2 1.5 %fusion.9 = f32[96,256]{1,0:T(8,128)S(1)} fusion(bf16[96,2048]{1,0:T(8,128)(2,1)S(1)} %reshape.66, bf16[1,1,2,2048,256]{4,3,2,1,0:T(8,128)(2,1)} %param.10), kind=kOutput, calls=%fused_computation.14 | convolution fusion | flops 100663296 | bytes 1540096 | tf_op jit(solution)/shard_map/dot_general | solution.py:37
  27.8 0.0 copy-done
  27.8 0.0 copy-start.1
  27.8 0.0 copy-start.2
  27.8 2.0 %convolution_convert_fusion = bf16[96,2048]{1,0:T(8,128)(2,1)S(1)} fusion(bf16[96,2048]{1,0:T(8,128)(2,1)S(1)} %reshape.66, bf16[1,1,256,2048]{3,2,1,0:T(8,128)(2,1)S(1)} %copy-done, bf16[1,1,2,2048,256]{4,3,2,1,0:T(8,128)(2,1)} %param.10, f32[96,256]{1,0:T(8,128)S(1)} %fusion.9), kind=kOutput, calls=%fused_computation.2 | convolution fusion | flops 201670656 | bytes 2981888 | tf_op jit(solution)/shard_map/dot_general | solution.py:40
  29.8 0.9 %reshape.67 = bf16[8,12,2048]{2,1,0:T(8,128)(2,1)} reshape(bf16[96,2048]{1,0:T(8,128)(2,1)S(1)} %convolution_convert_fusion) | data formatting | bytes 786432 | tf_op jit(solution)/shard_map/reshape | solution.py:61
  30.7 3.6 %all-to-all-start.1 = ((bf16[8,12,2048]{2,1,0:T(8,128)(2,1)}), bf16[8,12,2048]{2,1,0:T(8,128)(2,1)S(1)}, u32[]{:S(2)}, u32[]{:S(2)}) async-start(bf16[8,12,2048]{2,1,0:T(8,128)(2,1)} %reshape.67), calls=%async_computation.1 | async-start | bytes 1048576 | tf_op jit(solution)/shard_map/all_to_all | solution.py:62
  34.3 0.0 copy-done.1
  34.3 0.0 copy-done.2
  34.3 14.1 %all-to-all-done.1 = bf16[8,12,2048]{2,1,0:T(8,128)(2,1)S(1)} async-done(((bf16[8,12,2048]{2,1,0:T(8,128)(2,1)}), bf16[8,12,2048]{2,1,0:T(8,128)(2,1)S(1)}, u32[]{:S(2)}, u32[]{:S(2)}) %all-to-all-start.1) | async-done | bytes 393248 | tf_op jit(solution)/shard_map/all_to_all | solution.py:62
  48.5 0.1 reduce_sum.42
  48.6 0.6 %fusion.1 = bf16[1,128,2048]{2,1,0:T(8,128)(2,1)S(1)} fusion(bf16[2,12,2048]{2,1,0:T(8,128)(2,1)S(1)} %reduce_sum.42, f32[128,2]{0,1:T(2,128)S(1)} %select_reduce_fusion, s32[128,2]{0,1:T(2,128)S(1)} %convert_subtract_fusion, pred[128,2]{0,1:T(4,128)(4,1)S(1)} %get-tuple-element.5), kind=kOutput, calls=%fused_computation.3 | convolution fusion | flops 75768832 | bytes 624896 | tf_op jit(solution)/shard_map/tec,ecd->td/dot_general | solution.py:69
  49.2 0.1 collective-permute-start
  49.3 8.6 %collective-permute-done = bf16[1,128,2048]{2,1,0:T(8,128)(2,1)S(1)} collective-permute-done((bf16[1,128,2048]{2,1,0:T(8,128)(2,1)S(1)}, bf16[1,128,2048]{2,1,0:T(8,128)(2,1)S(1)}, u32[]{:S(2)}, u32[]{:S(2)}) %collective-permute-start) | collective-permute-done | bytes 524320 | tf_op jit(solution)/shard_map/ppermute | solution.py:15
  57.8 0.8 %copy.22 = bf16[1,128,2048]{2,1,0:T(8,128)(2,1)} copy(bf16[1,128,2048]{2,1,0:T(8,128)(2,1)S(1)} %collective-permute-done) | data formatting | bytes 1048576
  (7 shorter events, 0.1 us)
Async XLA Ops:
  0.0 27.8 %copy-start = (bf16[1,1,256,2048]{3,2,1,0:T(8,128)(2,1)S(1)}, bf16[1,1,256,2048]{3,2,1,0:T(8,128)(2,1)}, u32[]{:S(2)}) copy-start(bf16[1,1,256,2048]{3,2,1,0:T(8,128)(2,1)} %param.11) | copy-start | bytes 3145732
  27.8 6.5 %copy-start.1 = (f32[1,128,8]{1,2,0:T(8,128)S(1)}, f32[1,128,8]{1,2,0:T(8,128)}, u32[]{:S(2)}) copy-start(f32[1,128,8]{1,2,0:T(8,128)} %param.8) | copy-start | bytes 12292
  27.8 6.5 %copy-start.2 = (s32[1,128,8]{1,2,0:T(8,128)S(1)}, s32[1,128,8]{1,2,0:T(8,128)}, u32[]{:S(2)}) copy-start(s32[1,128,8]{1,2,0:T(8,128)} %param.9) | copy-start | bytes 12292
  30.7 17.8 %all-to-all-start.1 = ((bf16[8,12,2048]{2,1,0:T(8,128)(2,1)}), bf16[8,12,2048]{2,1,0:T(8,128)(2,1)S(1)}, u32[]{:S(2)}, u32[]{:S(2)}) async-start(bf16[8,12,2048]{2,1,0:T(8,128)(2,1)} %reshape.67), calls=%async_computation.1 | async-start | bytes 1048576 | tf_op jit(solution)/shard_map/all_to_all | solution.py:62
  49.2 8.7 %collective-permute-start = (bf16[1,128,2048]{2,1,0:T(8,128)(2,1)S(1)}, bf16[1,128,2048]{2,1,0:T(8,128)(2,1)S(1)}, u32[]{:S(2)}, u32[]{:S(2)}) collective-permute-start(bf16[1,128,2048]{2,1,0:T(8,128)(2,1)S(1)} %fusion.1), channel_id=1, source_target_pairs={{0,8},{8,16},{16,24},{24,0},{1,9},{9,17},{17,25},{25,1},{2,10},{10... | collective-permute-start | bytes 1572872 | tf_op jit(solution)/shard_map/ppermute | solution.py:15
where the time goes:
time: 59.1 us; the launch traced here: 58.6 us
  waiting for transfers between devices  22.7 us (38%)
  blocking collectives  21.6 us (37%)
  matrix products  5.51 us (9%)
  starting transfers between devices  3.65 us (6%)
  other arithmetic  3.09 us (5%)
  local copies, waits for them, and re-layouts  2 us (3%)
    all_to_all x1, blocking collectives, shards(): lax.all_to_all(fanned, ('dp', 'expert'), split_axis=0, concat_axis=0, til...  21.6 us
    all_to_all x1, waiting for transfers between devices, shards(): lax.all_to_all(partial_rows, ('dp', 'expert'), split_axis=0, concat_axis=...  14.1 us
    ppermute x1, waiting for transfers between devices, from_behind(): return lax.ppermute(value, axis, pairs)  8.59 us
    all_to_all x1, starting transfers between devices, shards(): lax.all_to_all(partial_rows, ('dp', 'expert'), split_axis=0, concat_axis=...  3.59 us
    dot_general x1, matrix products, expert_quarter(): jnp.dot(hidden, down_matrix, preferred_element_type=jnp.float32)  2 us
    dot_general x1, matrix products, expert_quarter(): jnp.dot(slot_rows, gate_up[0], preferred_element_type=jnp.float32)  1.53 us
    dot_general x1, matrix products, shards(): jnp.einsum('tec,td->ecd', slot_onehot, normed, preferred_element_type=jnp...  1.36 us
    reduce_sum x1, other arithmetic, normalize(): jnp.mean(widened * widened, axis=-1, keepdims=True) + epsilon  1.23 us
  transfers between devices with their start and end apart: 2, of which 2 were waited for; matrix products, arithmetic and copies ran while one was open for 0% of the time, Pallas kernels for 0%

commit v1 on v0

v1 whole, which is shorter than its diff:
```python
import functools

import jax
import jax.numpy as jnp
from jax import lax
from jax.experimental import pallas as pl
from jax.experimental.pallas import tpu as pltpu
from jax.sharding import PartitionSpec as P

CAP = 12
GROUP = 2 * CAP
epsilon = 1e-06
f32 = jnp.float32
bf16 = jnp.bfloat16
VMEM_LIMIT = 40 * 1024 * 1024


def row_tables(rows, lanes):
    row = lax.broadcasted_iota(jnp.int32, (rows, lanes), 0) % GROUP
    left = (row < 8) | ((row >= 16) & (row < 20))
    slot = jnp.where(row < 8, row, jnp.where(row < 20, row - 8, row - 12))
    return left, slot


def swap_halves(value):
    pieces = []
    for first in range(0, value.shape[0], GROUP):
        pieces.append(value[first + 8 : first + 16])
        pieces.append(value[first : first + 8])
        pieces.append(pltpu.roll(value[first + 16 : first + 24], 4, 0))
    return jnp.concatenate(pieces, axis=0)


def dot(left, right):
    return jnp.dot(left, right, preferred_element_type=f32)


def pack_kernel(base_ref, stream_ref, gain_ref, probs_ref, ids_ref, meta_ref, *packed_refs, held_count):
    ids = ids_ref[...]
    probs = probs_ref[...]
    weights = probs / jnp.sum(probs, axis=0, keepdims=True)
    tokens = ids.shape[1]
    half = stream_ref.shape[1] // 2
    chosen, coefficients = [], []
    for block in range(held_count):
        matches = ids == lax.rem(base_ref[0] + block, held_count)
        coefficients.append(jnp.sum(jnp.where(matches, weights, 0.0), axis=0, keepdims=True))
        chosen.append(jnp.sum(jnp.where(matches, 1.0, 0.0), axis=0, keepdims=True))
    padding = -held_count % 8
    stacked = jnp.concatenate(chosen + [jnp.zeros((padding, tokens), f32)] * (padding > 0), axis=0)
    earlier = lax.broadcasted_iota(jnp.int32, (tokens, tokens), 0) < lax.broadcasted_iota(
        jnp.int32, (tokens, tokens), 1
    )
    counted = dot(stacked.astype(bf16), jnp.where(earlier, 1.0, 0.0).astype(bf16))
    position = jnp.where(stacked > 0.5, counted, -1.0)
    rows = held_count * GROUP
    left, slot = row_tables(rows, tokens)
    spread = jnp.concatenate(
        [jnp.broadcast_to(position[e : e + 1], (GROUP, tokens)) for e in range(held_count)], axis=0
    )
    onehot = slot.astype(f32) == spread
    packed = dot(jnp.where(onehot & left, 1.0, 0.0).astype(bf16), stream_ref[:, :half])
    packed += dot(jnp.where(onehot & ~left, 1.0, 0.0).astype(bf16), stream_ref[:, half:])
    squares = packed * packed
    total = jnp.sum(squares + swap_halves(squares), axis=1, keepdims=True)
    inverse_rms = lax.rsqrt(total / (2 * half) + epsilon)
    gain = gain_ref[...].astype(f32)
    left, _ = row_tables(rows, half)
    normed = packed * inverse_rms * jnp.where(left, gain[:, :half], gain[:, half:])
    per_ref = rows // len(packed_refs)
    for index, ref in enumerate(packed_refs):
        ref[...] = normed[index * per_ref : (index + 1) * per_ref].astype(bf16)
    lines = []
    for block in range(held_count):
        rest = coefficients[block]
        for _ in range(3):
            piece = rest.astype(bf16).astype(f32)
            lines.append(piece)
            rest = rest - piece
        lines.append(position[block : block + 1])
    table = jnp.concatenate(lines, axis=0)
    meta_ref[...] = table.astype(bf16)


def pack(stream, gain, probs, ids, base, held_count, outputs):
    tokens, width = stream.shape
    rows = held_count * GROUP // outputs
    whole = pl.BlockSpec(memory_space=pltpu.VMEM)
    return pl.pallas_call(
        functools.partial(pack_kernel, held_count=held_count),
        out_shape=[jax.ShapeDtypeStruct((4 * held_count, tokens), bf16)]
        + [jax.ShapeDtypeStruct((rows, width // 2), bf16)] * outputs,
        in_specs=[pl.BlockSpec(memory_space=pltpu.SMEM)] + [whole] * 4,
        out_specs=[whole] * (1 + outputs),
        compiler_params=pltpu.CompilerParams(vmem_limit_bytes=VMEM_LIMIT),
        cost_estimate=pl.CostEstimate(flops=2 * rows * tokens * width, bytes_accessed=2 * tokens * width, transcendentals=0),
    )(base, stream, gain, probs, ids)


def expert_rows(value, gate_ref, up_ref, down_ref):
    half = value.shape[1]
    value = value.astype(f32)
    swapped = swap_halves(value)
    left, _ = row_tables(*value.shape)
    first = jnp.where(left, value, swapped).astype(bf16)
    second = jnp.where(left, swapped, value).astype(bf16)
    gate = dot(first, gate_ref[:half]) + dot(second, gate_ref[half:])
    up = dot(first, up_ref[:half]) + dot(second, up_ref[half:])
    hidden = (gate / (1.0 + jnp.exp(-gate)) * up).astype(bf16)
    result = dot(hidden, down_ref[...])
    return jnp.where(left, result[:, :half], result[:, half:])


def expert_kernel(gate_up_ref, down_ref, *refs, count):
    value = jnp.concatenate([ref[...].astype(f32) for ref in refs[:count]], axis=0)
    result = expert_rows(value, gate_up_ref.at[0], gate_up_ref.at[1], down_ref)
    first = 0
    for ref in refs[count:]:
        ref[...] = result[first : first + ref.shape[0]].astype(bf16)
        first += ref.shape[0]


def expert_quarter(blocks, out_rows, gate_up, down):
    width = blocks[0].shape[1]
    rows = sum(block.shape[0] for block in blocks)
    whole = pl.BlockSpec(memory_space=pltpu.VMEM)
    return pl.pallas_call(
        functools.partial(expert_kernel, count=len(blocks)),
        out_shape=[jax.ShapeDtypeStruct((count, width), bf16) for count in out_rows],
        in_specs=[whole] * (2 + len(blocks)),
        out_specs=[whole] * len(out_rows),
        compiler_params=pltpu.CompilerParams(vmem_limit_bytes=VMEM_LIMIT),
        cost_estimate=pl.CostEstimate(
            flops=rows * 3 * down.size, bytes_accessed=2 * (gate_up.size + down.size), transcendentals=rows * down.shape[0]
        ),
    )(gate_up, down, *blocks)


def many_kernel(gate_up_ref, down_ref, in_ref, out_ref):
    out_ref[...] = expert_rows(in_ref[...], gate_up_ref.at[0], gate_up_ref.at[1], down_ref).astype(bf16)


def expert_quarter_many(block, gate_up, down):
    rows, width = block.shape
    step = GROUP * 4 if rows % (GROUP * 4) == 0 else rows
    return pl.pallas_call(
        many_kernel,
        grid=(rows // step,),
        out_shape=jax.ShapeDtypeStruct((rows, width), bf16),
        in_specs=[
            pl.BlockSpec(gate_up.shape, lambda i: (0, 0, 0)),
            pl.BlockSpec(down.shape, lambda i: (0, 0)),
            pl.BlockSpec((step, width), lambda i: (i, 0)),
        ],
        out_specs=pl.BlockSpec((step, width), lambda i: (i, 0)),
        compiler_params=pltpu.CompilerParams(vmem_limit_bytes=VMEM_LIMIT),
    )(gate_up, down, block)


def mix_kernel(meta_ref, *refs, held_count):
    rows_refs, out_ref = refs[:-1], refs[-1]
    half = out_ref.shape[1] // 2
    tokens = out_ref.shape[0]
    meta = meta_ref[:, :tokens].astype(f32)
    left, slot = row_tables(GROUP, tokens)
    blocks = []
    for ref in rows_refs:
        value = ref[...].astype(f32)
        for first in range(0, value.shape[0] // GROUP * GROUP, GROUP):
            blocks.append(value[first : first + GROUP])
    values = jnp.concatenate(blocks[:held_count], axis=0).astype(bf16)
    sides = [jnp.zeros((tokens, half), f32)] * 2
    for piece in range(3):
        tables = [[], []]
        for block in range(held_count):
            position = meta[4 * block + 3 : 4 * block + 4]
            share = meta[4 * block + piece : 4 * block + piece + 1]
            held = slot.astype(f32) == position
            tables[0].append(jnp.where(held & left, share, 0.0))
            tables[1].append(jnp.where(held & ~left, share, 0.0))
        for side in range(2):
            table = jnp.concatenate(tables[side], axis=0)
            sides[side] = sides[side] + dot(table.T.astype(bf16), values)
    out_ref[:, :half] = sides[0].astype(bf16)
    out_ref[:, half:] = sides[1].astype(bf16)


def mix(meta, blocks, tokens, held_count):
    width = blocks[0].shape[1]
    whole = pl.BlockSpec(memory_space=pltpu.VMEM)
    return pl.pallas_call(
        functools.partial(mix_kernel, held_count=held_count),
        out_shape=jax.ShapeDtypeStruct((tokens, 2 * width), bf16),
        in_specs=[whole] * (1 + len(blocks)),
        out_specs=whole,
        compiler_params=pltpu.CompilerParams(vmem_limit_bytes=VMEM_LIMIT),
    )(meta, *blocks)


def move(value, axes, target):
    sizes = [lax.axis_size(axis) for axis in axes]
    pairs = []
    total = 1
    for size in sizes:
        total *= size
    for source in range(total):
        rest, place = source, []
        for size in reversed(sizes):
            place.insert(0, rest % size)
            rest //= size
        index = 0
        for size, coordinate in zip(sizes, target(*place)):
            index = index * size + coordinate % size
        pairs.append((source, index))
    return lax.ppermute(value, axes if len(axes) > 1 else axes[0], pairs)


def across(value, step):
    return move(value, ("dp",), lambda q: (q ^ step,))


def added(values):
    total = values[0].astype(f32)
    for value in values[1:]:
        total = total + value.astype(f32)
    return total.astype(bf16)


def pair_shards(stream, gain, probs, ids, gate_up, down):
    base = lax.axis_index("expert").astype(jnp.int32).reshape(1)
    meta, own, other = pack(stream, gain, probs, ids, base, 2, 2)
    other = move(other, ("expert",), lambda e: (e ^ 1,))
    own3, own2 = across(own, 3), across(own, 2)
    other3, other2 = across(other, 3), across(other, 2)
    both1 = across(jnp.concatenate([own, other], axis=0), 1)
    part0, part3 = expert_quarter([own, other, own3, other3], [2 * GROUP] * 2, gate_up, down)
    back3 = across(part3, 3)
    part2, part1 = expert_quarter([own2, other2, both1], [2 * GROUP] * 2, gate_up, down)
    back2, back1 = across(part2, 2), across(part1, 1)
    summed = added([part0, back1, back2, back3])
    tagged = jnp.concatenate(
        [summed[:GROUP], jnp.pad(meta, ((0, 0), (0, summed.shape[1] - meta.shape[1])))], axis=0
    )
    tagged = move(tagged, ("section",), lambda s: (s + 1,))
    crossed = move(summed[GROUP:], ("section", "expert"), lambda s, e: (s + 1, e ^ 1))
    return mix(tagged[GROUP:], [tagged[:GROUP], crossed], stream.shape[0], 2)


def many_shards(stream, gain, probs, ids, gate_up, down):
    held_count = lax.axis_size("expert")
    group_count = lax.axis_size("dp")
    base = jnp.zeros((1,), jnp.int32)
    meta, packed = pack(stream, gain, probs, ids, base, held_count, 1)
    meta = move(meta, ("section",), lambda s: (s + 1,))
    shape = packed.shape
    split = (held_count, GROUP, shape[1])

    def exchanged(value):
        return lax.all_to_all(value.reshape(split), "expert", split_axis=0, concat_axis=0, tiled=True).reshape(shape)

    def shifted(value, step):
        return move(value, ("dp",), lambda q: (q + step,))

    received = exchanged(packed)
    parts = [expert_quarter_many(received, gate_up, down)]
    for step in range(1, group_count):
        parts.append(shifted(expert_quarter_many(shifted(received, step), gate_up, down), -step))
    summed = move(exchanged(added(parts)), ("section",), lambda s: (s + 1,))
    return mix(meta, [summed], stream.shape[0], held_count)


def shards(stream, norm_gain, gate_probs, expert_ids, gate_up_weight, down_weight):
    paired = lax.axis_size("expert") == 2 and lax.axis_size("dp") == 4
    body = pair_shards if paired else many_shards
    return body(
        stream[0], norm_gain, gate_probs[0].T, expert_ids[0].T, gate_up_weight[0, 0], down_weight[0, 0]
    )[None]


def solution(mesh):
    in_specs = (
        P("section", ("dp", "expert"), None),
        P("section", None),
        P("section", ("dp", "expert"), None),
        P("section", ("dp", "expert"), None),
        P("section", "expert", None, None, "dp"),
        P("section", "expert", "dp", None),
    )
    out_specs = P("section", ("dp", "expert"), None)
    return jax.shard_map(shards, mesh=mesh, in_specs=in_specs, out_specs=out_specs, check_vma=False)
```

time: 59.1 us -> 39.9 us (0.68)
  blocking collectives: 21.6 us -> 0 us
  starting transfers between devices: 3.65 us -> 19.2 us
  waiting for transfers between devices: 22.7 us -> 10.7 us
  matrix products: 5.51 us -> 0 us
  local copies, waits for them, and re-layouts: 2 us -> 5.95 us
  Pallas kernels: 0 us -> 3.33 us
  other arithmetic: 3.09 us -> 0.07 us
    all_to_all x1 -> x0, blocking collectives: 21.6 us -> none  [shards(): lax.all_to_all(fanned, ('dp', 'expert'), split_axis=0, concat_axis=0, til...]
    ppermute x1 -> x11, starting transfers between devices: 0.06 us -> 19.2 us  [move(): return lax.ppermute(value, axes if len(axes) > 1 else axes[0], pairs)]
    all_to_all x1 -> x0, waiting for transfers between devices: 14.1 us -> none  [shards(): lax.all_to_all(partial_rows, ('dp', 'expert'), split_axis=0, concat_axis=...]
    dot_general x4 -> x0, matrix products: 5.51 us -> none  [the longest x1 2 us: expert_quarter(): jnp.dot(hidden, down_matrix, preferred_element_type=jnp.float32)]
    unnamed x7 -> x16, local copies, waits for them, and re-layouts: 0.81 us -> 5.93 us
    all_to_all x1 -> x0, starting transfers between devices: 3.59 us -> none  [shards(): lax.all_to_all(partial_rows, ('dp', 'expert'), split_axis=0, concat_axis=...]
    pallas_call x0 -> x4, Pallas kernels: none -> 3.33 us  [the longest x2 1.47 us: expert_quarter(): pl.pallas_call(functools.partial(expert_kernel, count=len(blocks)), out_s...]
    ppermute x1 -> x11, waiting for transfers between devices: 8.59 us -> 10.7 us  [move(): return lax.ppermute(value, axes if len(axes) > 1 else axes[0], pairs)]
  transfers between devices with their start and end apart: 2 -> 11, of which waited for: 2 -> 7; matrix products, arithmetic and copies ran while one was open for 0% -> 0% of each run, Pallas kernels for 0% -> 4%
where the time goes in v1:
time: 39.9 us; the launch traced here: 39.3 us
  starting transfers between devices  19.2 us (48%)
  waiting for transfers between devices  10.7 us (27%)
  local copies, waits for them, and re-layouts  5.95 us (15%)
  Pallas kernels  3.33 us (8%)
    ppermute x11, starting transfers between devices, move(): return lax.ppermute(value, axes if len(axes) > 1 else axes[0], pairs)  19.2 us
    ppermute x11, waiting for transfers between devices, move(): return lax.ppermute(value, axes if len(axes) > 1 else axes[0], pairs)  10.7 us
    unnamed x16, local copies, waits for them, and re-layouts  5.93 us
    pallas_call x2, Pallas kernels, expert_quarter(): pl.pallas_call(functools.partial(expert_kernel, count=len(blocks)), out_s...  1.47 us
    pallas_call x1, Pallas kernels, mix(): pl.pallas_call(functools.partial(mix_kernel, held_count=held_count), out_...  1.43 us
  transfers between devices with their start and end apart: 11, of which 7 were waited for; matrix products, arithmetic and copies ran while one was open for 0% of the time, Pallas kernels for 4%

profile of v1, /device:TPU:0, one launch (start us, length us, event | category | flops | bytes accessed | tf_op | source)
XLA Modules:
  0.0 39.3 jit_solution(13597679325046027021)
XLA Ops:
  0.0 0.0 copy-start.4
  0.0 1.0 %copy-done.4 = bf16[1,128,2048]{2,1,0:T(8,128)(2,1)S(1)} copy-done((bf16[1,128,2048]{2,1,0:T(8,128)(2,1)S(1)}, bf16[1,128,2048]{2,1,0:T(8,128)(2,1)}, u32[]{:S(2)}) %copy-start.4) | copy-done | bytes 524312
  1.0 0.0 copy-start.5
  1.0 0.7 %copy-done.5 = bf16[1,2048]{1,0:T(2,128)(2,1)S(1)} copy-done((bf16[1,2048]{1,0:T(2,128)(2,1)S(1)}, bf16[1,2048]{1,0:T(2,128)(2,1)}, u32[]{:S(2)}) %copy-start.5) | copy-done | bytes 4120
  1.7 0.0 copy-start.6
  1.7 0.7 %copy-done.6 = f32[1,128,8]{1,2,0:T(8,128)S(1)} copy-done((f32[1,128,8]{1,2,0:T(8,128)S(1)}, f32[1,128,8]{1,2,0:T(8,128)}, u32[]{:S(2)}) %copy-start.6) | copy-done | bytes 4120
  2.4 0.0 copy-start.7
  2.4 0.7 %copy-done.7 = s32[1,128,8]{1,2,0:T(8,128)S(1)} copy-done((s32[1,128,8]{1,2,0:T(8,128)S(1)}, s32[1,128,8]{1,2,0:T(8,128)}, u32[]{:S(2)}) %copy-start.7) | copy-done | bytes 4120
  3.1 0.4 %shard_map.64 = (bf16[8,128]{1,0:T(8,128)(2,1)S(1)}, bf16[24,1024]{1,0:T(8,128)(2,1)S(1)}, bf16[24,1024]{1,0:T(8,128)(2,1)S(1)}) custom-call(s32[1]{0:T(128)} %bitcast.2.base_ref, bf16[128,2048]{1,0:T(8,128)(2,1)S(1)} %bitcast.15, bf16[1,2048]{1,0:T(2,128)(2,1)S(1)} %copy-done.5, f32[8,128]{1,0:T(8,128)S(1)} %bitcast.16, s32[8,128]{1,0:T(8,128)S(1)} %bitcast.17), custom_call_target="tpu_custom_call" | custom-call | flops 12582912 | bytes 524288 | tf_op jit(solution)/shard_map/pallas_call | solution.py:89
  3.6 3.0 %collective-permute-start = (bf16[24,1024]{1,0:T(8,128)(2,1)S(1)}, bf16[24,1024]{1,0:T(8,128)(2,1)S(1)}, u32[]{:S(2)}, u32[]{:S(2)}) collective-permute-start(bf16[24,1024]{1,0:T(8,128)(2,1)S(1)} %get-tuple-element.13), channel_id=1, source_target_pairs={{0,1},{1,0},{2,3},{3,2},{4,5},{5,4},{6,7},{7,6},{8,9},{9,8},{10,11... | collective-permute-start | bytes 147464 | tf_op jit(solution)/shard_map/ppermute | solution.py:215
  6.6 2.1 %collective-permute-done.refs_1_ = bf16[24,1024]{1,0:T(8,128)(2,1)S(1)} collective-permute-done((bf16[24,1024]{1,0:T(8,128)(2,1)S(1)}, bf16[24,1024]{1,0:T(8,128)(2,1)S(1)}, u32[]{:S(2)}, u32[]{:S(2)}) %collective-permute-start) | collective-permute-done | bytes 49184 | tf_op jit(solution)/shard_map/ppermute | solution.py:215
  8.6 2.2 %collective-permute-start.5 = (bf16[48,1024]{1,0:T(8,128)(2,1)S(1)}, bf16[48,1024]{1,0:T(8,128)(2,1)S(1)}, u32[]{:S(2)}, u32[]{:S(2)}) collective-permute-start(bf16[48,1024]{1,0:T(8,128)(2,1)S(1)} %pad_maximum_fusion), channel_id=1, source_target_pairs={{0,2},{2,0},{4,6},{6,4},{1,3},{3,1},{5,7},{7,5},{8,10},{10,8},{12,... | collective-permute-start | bytes 294920 | tf_op jit(solution)/shard_map/ppermute | solution.py:215
  10.8 2.5 %collective-permute-start.1 = (bf16[24,1024]{1,0:T(8,128)(2,1)S(1)}, bf16[24,1024]{1,0:T(8,128)(2,1)S(1)}, u32[]{:S(2)}, u32[]{:S(2)}) collective-permute-start(bf16[24,1024]{1,0:T(8,128)(2,1)S(1)} %get-tuple-element.12.refs_0_), channel_id=1, source_target_pairs={{0,6},{2,4},{4,2},{6,0},{1,7},{3,5},{5,3},{7,1},{8,14},{10,12},{12... | collective-permute-start | bytes 147464 | tf_op jit(solution)/shard_map/ppermute | solution.py:215
  13.3 1.3 %collective-permute-start.2 = (bf16[24,1024]{1,0:T(8,128)(2,1)S(1)}, bf16[24,1024]{1,0:T(8,128)(2,1)S(1)}, u32[]{:S(2)}, u32[]{:S(2)}) collective-permute-start(bf16[24,1024]{1,0:T(8,128)(2,1)S(1)} %collective-permute-done.refs_1_), channel_id=1, source_target_pairs={{0,6},{2,4},{4,2},{6,0},{1,7},{3,5},{5,3},{7,1},{8,14},{10,12},{12... | collective-permute-start | bytes 147464 | tf_op jit(solution)/shard_map/ppermute | solution.py:215
  14.6 0.8 %collective-permute-start.3 = (bf16[24,1024]{1,0:T(8,128)(2,1)S(1)}, bf16[24,1024]{1,0:T(8,128)(2,1)S(1)}, u32[]{:S(2)}, u32[]{:S(2)}) collective-permute-start(bf16[24,1024]{1,0:T(8,128)(2,1)S(1)} %get-tuple-element.12.refs_0_), channel_id=1, source_target_pairs={{0,4},{2,6},{4,0},{6,2},{1,5},{3,7},{5,1},{7,3},{8,12},{10,14},{12... | collective-permute-start | bytes 147464 | tf_op jit(solution)/shard_map/ppermute | solution.py:215
  15.4 2.1 %collective-permute-start.4 = (bf16[24,1024]{1,0:T(8,128)(2,1)S(1)}, bf16[24,1024]{1,0:T(8,128)(2,1)S(1)}, u32[]{:S(2)}, u32[]{:S(2)}) collective-permute-start(bf16[24,1024]{1,0:T(8,128)(2,1)S(1)} %collective-permute-done.refs_1_), channel_id=1, source_target_pairs={{0,4},{2,6},{4,0},{6,2},{1,5},{3,7},{5,1},{7,3},{8,12},{10,14},{12... | collective-permute-start | bytes 147464 | tf_op jit(solution)/shard_map/ppermute | solution.py:215
  17.6 0.0 collective-permute-done.1.refs_2_
  17.6 1.8 %collective-permute-done.2.refs_3_ = bf16[24,1024]{1,0:T(8,128)(2,1)S(1)} collective-permute-done((bf16[24,1024]{1,0:T(8,128)(2,1)S(1)}, bf16[24,1024]{1,0:T(8,128)(2,1)S(1)}, u32[]{:S(2)}, u32[]{:S(2)}) %collective-permute-start.2) | collective-permute-done | bytes 49184 | tf_op jit(solution)/shard_map/ppermute | solution.py:215
  19.3 0.0 copy-start
  19.3 1.6 %copy-done = bf16[1,1,2,2048,256]{4,3,2,1,0:T(8,128)(2,1)S(1)} copy-done((bf16[1,1,2,2048,256]{4,3,2,1,0:T(8,128)(2,1)S(1)}, bf16[1,1,2,2048,256]{4,3,2,1,0:T(8,128)(2,1)}, u32[]{:S(2)}) %copy-start) | copy-done | bytes 2097176
  20.9 0.0 copy-start.2
  20.9 1.2 %copy-done.2 = bf16[1,1,256,2048]{3,2,1,0:T(8,128)(2,1)S(1)} copy-done((bf16[1,1,256,2048]{3,2,1,0:T(8,128)(2,1)S(1)}, bf16[1,1,256,2048]{3,2,1,0:T(8,128)(2,1)}, u32[]{:S(2)}) %copy-start.2) | copy-done | bytes 1048600
  22.1 0.0 copy-start.1
  22.1 0.0 copy-start.3
  22.2 0.7 %shard_map.65 = (bf16[48,1024]{1,0:T(8,128)(2,1)S(1)}, bf16[48,1024]{1,0:T(8,128)(2,1)S(1)}) custom-call(bf16[2,2048,256]{2,1,0:T(8,128)(2,1)S(1)} %bitcast.11, bf16[256,2048]{1,0:T(8,128)(2,1)S(1)} %bitcast.13, bf16[24,1024]{1,0:T(8,128)(2,1)S(1)} %get-tuple-element.12.refs_0_, bf16[24,1024]{1,0:T(8,128)(2,1)S(1)} %collective-permute-done.refs_1_, ...), custom_call_target="tpu_custom_call" | custom-call | flops 150994944 | bytes 3145728 | tf_op jit(solution)/shard_map/pallas_call | solution.py:127
  22.9 1.3 %collective-permute-start.8 = (bf16[48,1024]{1,0:T(8,128)(2,1)S(1)}, bf16[48,1024]{1,0:T(8,128)(2,1)S(1)}, u32[]{:S(2)}, u32[]{:S(2)}) collective-permute-start(bf16[48,1024]{1,0:T(8,128)(2,1)S(1)} %get-tuple-element.17), channel_id=1, source_target_pairs={{0,6},{2,4},{4,2},{6,0},{1,7},{3,5},{5,3},{7,1},{8,14},{10,12},{12... | collective-permute-start | bytes 294920 | tf_op jit(solution)/shard_map/ppermute | solution.py:215
  24.2 0.0 collective-permute-done.3.refs_0_
  24.2 0.0 collective-permute-done.4.refs_1_
  24.2 0.0 collective-permute-done.5.refs_2_
  24.2 0.0 copy-done.1
  24.2 0.0 copy-done.3
  24.2 0.7 %shard_map.66 = (bf16[48,1024]{1,0:T(8,128)(2,1)S(1)}, bf16[48,1024]{1,0:T(8,128)(2,1)S(1)}) custom-call(bf16[2,2048,256]{2,1,0:T(8,128)(2,1)S(1)} %bitcast.12, bf16[256,2048]{1,0:T(8,128)(2,1)S(1)} %bitcast.14, bf16[24,1024]{1,0:T(8,128)(2,1)S(1)} %collective-permute-done.3.refs_0_, bf16[24,1024]{1,0:T(8,128)(2,1)S(1)} %collective-permute-done.4.refs_1_, ...), custom_call_target="tpu_custom_call" | custom-call | flops 150994944 | bytes 3145728 | tf_op jit(solution)/shard_map/pallas_call | solution.py:127
  25.0 1.7 %collective-permute-start.6 = (bf16[48,1024]{1,0:T(8,128)(2,1)S(1)}, bf16[48,1024]{1,0:T(8,128)(2,1)S(1)}, u32[]{:S(2)}, u32[]{:S(2)}) collective-permute-start(bf16[48,1024]{1,0:T(8,128)(2,1)S(1)} %get-tuple-element.15), channel_id=1, source_target_pairs={{0,2},{2,0},{4,6},{6,4},{1,3},{3,1},{5,7},{7,5},{8,10},{10,8},{12,... | collective-permute-start | bytes 294920 | tf_op jit(solution)/shard_map/ppermute | solution.py:215
  26.7 1.5 %collective-permute-start.7 = (bf16[48,1024]{1,0:T(8,128)(2,1)S(1)}, bf16[48,1024]{1,0:T(8,128)(2,1)S(1)}, u32[]{:S(2)}, u32[]{:S(2)}) collective-permute-start(bf16[48,1024]{1,0:T(8,128)(2,1)S(1)} %get-tuple-element.16), channel_id=1, source_target_pairs={{0,4},{2,6},{4,0},{6,2},{1,5},{3,7},{5,1},{7,3},{8,12},{10,14},{12... | collective-permute-start | bytes 294920 | tf_op jit(solution)/shard_map/ppermute | solution.py:215
  28.2 1.3 %collective-permute-done.8 = bf16[48,1024]{1,0:T(8,128)(2,1)S(1)} collective-permute-done((bf16[48,1024]{1,0:T(8,128)(2,1)S(1)}, bf16[48,1024]{1,0:T(8,128)(2,1)S(1)}, u32[]{:S(2)}, u32[]{:S(2)}) %collective-permute-start.8) | collective-permute-done | bytes 98336 | tf_op jit(solution)/shard_map/ppermute | solution.py:215
  29.5 1.0 %collective-permute-done.6 = bf16[48,1024]{1,0:T(8,128)(2,1)S(1)} collective-permute-done((bf16[48,1024]{1,0:T(8,128)(2,1)S(1)}, bf16[48,1024]{1,0:T(8,128)(2,1)S(1)}, u32[]{:S(2)}, u32[]{:S(2)}) %collective-permute-start.6) | collective-permute-done | bytes 98336 | tf_op jit(solution)/shard_map/ppermute | solution.py:215
  30.5 2.8 %collective-permute-done.7 = bf16[48,1024]{1,0:T(8,128)(2,1)S(1)} collective-permute-done((bf16[48,1024]{1,0:T(8,128)(2,1)S(1)}, bf16[48,1024]{1,0:T(8,128)(2,1)S(1)}, u32[]{:S(2)}, u32[]{:S(2)}) %collective-permute-start.7) | collective-permute-done | bytes 98336 | tf_op jit(solution)/shard_map/ppermute | solution.py:215
  33.3 0.1 add_convert_fusion
  33.4 0.1 collective-permute-start.9
  33.4 2.7 %collective-permute-start.10 = (bf16[24,1024]{1,0:T(8,128)(2,1)S(1)}, bf16[24,1024]{1,0:T(8,128)(2,1)S(1)}, u32[]{:S(2)}, u32[]{:S(2)}) collective-permute-start(bf16[24,1024]{1,0:T(8,128)(2,1)S(1)} %get-tuple-element.19), channel_id=1, source_target_pairs={{0,9},{1,8},{8,17},{9,16},{16,25},{17,24},{24,1},{25,0},{2,11},{3,... | collective-permute-start | bytes 147464 | tf_op jit(solution)/shard_map/ppermute | solution.py:215
  36.2 1.0 %collective-permute-done.9 = bf16[32,1024]{1,0:T(8,128)(2,1)S(1)} collective-permute-done((bf16[32,1024]{1,0:T(8,128)(2,1)S(1)}, bf16[32,1024]{1,0:T(8,128)(2,1)S(1)}, u32[]{:S(2)}, u32[]{:S(2)}) %collective-permute-start.9) | collective-permute-done | bytes 65568 | tf_op jit(solution)/shard_map/ppermute | solution.py:215
  37.1 0.8 %collective-permute-done.10.refs_1_ = bf16[24,1024]{1,0:T(8,128)(2,1)S(1)} collective-permute-done((bf16[24,1024]{1,0:T(8,128)(2,1)S(1)}, bf16[24,1024]{1,0:T(8,128)(2,1)S(1)}, u32[]{:S(2)}, u32[]{:S(2)}) %collective-permute-start.10) | collective-permute-done | bytes 49184 | tf_op jit(solution)/shard_map/ppermute | solution.py:215
  37.9 1.4 %shard_map.67 = bf16[128,2048]{1,0:T(8,128)(2,1)} custom-call(bf16[8,1024]{1,0:T(8,128)(2,1)S(1)} %slice.17.meta_ref, bf16[24,1024]{1,0:T(8,128)(2,1)S(1)} %slice.18.refs_0_, bf16[24,1024]{1,0:T(8,128)(2,1)S(1)} %collective-permute-done.10.refs_1_), custom_call_target="tpu_custom_call" | custom-call | tf_op jit(solution)/shard_map/pallas_call | solution.py:191
  (5 shorter events, 0.0 us)
Async XLA Ops:
  0.0 1.0 %copy-start.4 = (bf16[1,128,2048]{2,1,0:T(8,128)(2,1)S(1)}, bf16[1,128,2048]{2,1,0:T(8,128)(2,1)}, u32[]{:S(2)}) copy-start(bf16[1,128,2048]{2,1,0:T(8,128)(2,1)} %param.6) | copy-start | bytes 1572868
  1.0 0.7 %copy-start.5 = (bf16[1,2048]{1,0:T(2,128)(2,1)S(1)}, bf16[1,2048]{1,0:T(2,128)(2,1)}, u32[]{:S(2)}) copy-start(bf16[1,2048]{1,0:T(2,128)(2,1)} %gain_ref.1) | copy-start | bytes 12292
  1.7 0.7 %copy-start.6 = (f32[1,128,8]{1,2,0:T(8,128)S(1)}, f32[1,128,8]{1,2,0:T(8,128)}, u32[]{:S(2)}) copy-start(f32[1,128,8]{1,2,0:T(8,128)} %param.8) | copy-start | bytes 12292
  2.4 0.7 %copy-start.7 = (s32[1,128,8]{1,2,0:T(8,128)S(1)}, s32[1,128,8]{1,2,0:T(8,128)}, u32[]{:S(2)}) copy-start(s32[1,128,8]{1,2,0:T(8,128)} %param.9) | copy-start | bytes 12292
  3.6 5.1 %collective-permute-start = (bf16[24,1024]{1,0:T(8,128)(2,1)S(1)}, bf16[24,1024]{1,0:T(8,128)(2,1)S(1)}, u32[]{:S(2)}, u32[]{:S(2)}) collective-permute-start(bf16[24,1024]{1,0:T(8,128)(2,1)S(1)} %get-tuple-element.13), channel_id=1, source_target_pairs={{0,1},{1,0},{2,3},{3,2},{4,5},{5,4},{6,7},{7,6},{8,9},{9,8},{10,11... | collective-permute-start | bytes 147464 | tf_op jit(solution)/shard_map/ppermute | solution.py:215
  8.6 15.6 %collective-permute-start.5 = (bf16[48,1024]{1,0:T(8,128)(2,1)S(1)}, bf16[48,1024]{1,0:T(8,128)(2,1)S(1)}, u32[]{:S(2)}, u32[]{:S(2)}) collective-permute-start(bf16[48,1024]{1,0:T(8,128)(2,1)S(1)} %pad_maximum_fusion), channel_id=1, source_target_pairs={{0,2},{2,0},{4,6},{6,4},{1,3},{3,1},{5,7},{7,5},{8,10},{10,8},{12,... | collective-permute-start | bytes 294920 | tf_op jit(solution)/shard_map/ppermute | solution.py:215
  10.8 6.8 %collective-permute-start.1 = (bf16[24,1024]{1,0:T(8,128)(2,1)S(1)}, bf16[24,1024]{1,0:T(8,128)(2,1)S(1)}, u32[]{:S(2)}, u32[]{:S(2)}) collective-permute-start(bf16[24,1024]{1,0:T(8,128)(2,1)S(1)} %get-tuple-element.12.refs_0_), channel_id=1, source_target_pairs={{0,6},{2,4},{4,2},{6,0},{1,7},{3,5},{5,3},{7,1},{8,14},{10,12},{12... | collective-permute-start | bytes 147464 | tf_op jit(solution)/shard_map/ppermute | solution.py:215
  13.3 6.0 %collective-permute-start.2 = (bf16[24,1024]{1,0:T(8,128)(2,1)S(1)}, bf16[24,1024]{1,0:T(8,128)(2,1)S(1)}, u32[]{:S(2)}, u32[]{:S(2)}) collective-permute-start(bf16[24,1024]{1,0:T(8,128)(2,1)S(1)} %collective-permute-done.refs_1_), channel_id=1, source_target_pairs={{0,6},{2,4},{4,2},{6,0},{1,7},{3,5},{5,3},{7,1},{8,14},{10,12},{12... | collective-permute-start | bytes 147464 | tf_op jit(solution)/shard_map/ppermute | solution.py:215
  14.6 9.6 %collective-permute-start.3 = (bf16[24,1024]{1,0:T(8,128)(2,1)S(1)}, bf16[24,1024]{1,0:T(8,128)(2,1)S(1)}, u32[]{:S(2)}, u32[]{:S(2)}) collective-permute-start(bf16[24,1024]{1,0:T(8,128)(2,1)S(1)} %get-tuple-element.12.refs_0_), channel_id=1, source_target_pairs={{0,4},{2,6},{4,0},{6,2},{1,5},{3,7},{5,1},{7,3},{8,12},{10,14},{12... | collective-permute-start | bytes 147464 | tf_op jit(solution)/shard_map/ppermute | solution.py:215
  15.4 8.8 %collective-permute-start.4 = (bf16[24,1024]{1,0:T(8,128)(2,1)S(1)}, bf16[24,1024]{1,0:T(8,128)(2,1)S(1)}, u32[]{:S(2)}, u32[]{:S(2)}) collective-permute-start(bf16[24,1024]{1,0:T(8,128)(2,1)S(1)} %collective-permute-done.refs_1_), channel_id=1, source_target_pairs={{0,4},{2,6},{4,0},{6,2},{1,5},{3,7},{5,1},{7,3},{8,12},{10,14},{12... | collective-permute-start | bytes 147464 | tf_op jit(solution)/shard_map/ppermute | solution.py:215
  19.3 1.6 %copy-start = (bf16[1,1,2,2048,256]{4,3,2,1,0:T(8,128)(2,1)S(1)}, bf16[1,1,2,2048,256]{4,3,2,1,0:T(8,128)(2,1)}, u32[]{:S(2)}) copy-start(bf16[1,1,2,2048,256]{4,3,2,1,0:T(8,128)(2,1)} %param.10) | copy-start | bytes 6291460
  20.9 1.2 %copy-start.2 = (bf16[1,1,256,2048]{3,2,1,0:T(8,128)(2,1)S(1)}, bf16[1,1,256,2048]{3,2,1,0:T(8,128)(2,1)}, u32[]{:S(2)}) copy-start(bf16[1,1,256,2048]{3,2,1,0:T(8,128)(2,1)} %param.11) | copy-start | bytes 3145732
  22.1 2.1 %copy-start.1 = (bf16[1,1,2,2048,256]{4,3,2,1,0:T(8,128)(2,1)S(1)}, bf16[1,1,2,2048,256]{4,3,2,1,0:T(8,128)(2,1)}, u32[]{:S(2)}) copy-start(bf16[1,1,2,2048,256]{4,3,2,1,0:T(8,128)(2,1)} %param.10) | copy-start | bytes 6291460
  22.1 2.1 %copy-start.3 = (bf16[1,1,256,2048]{3,2,1,0:T(8,128)(2,1)S(1)}, bf16[1,1,256,2048]{3,2,1,0:T(8,128)(2,1)}, u32[]{:S(2)}) copy-start(bf16[1,1,256,2048]{3,2,1,0:T(8,128)(2,1)} %param.11) | copy-start | bytes 3145732
  22.9 6.6 %collective-permute-start.8 = (bf16[48,1024]{1,0:T(8,128)(2,1)S(1)}, bf16[48,1024]{1,0:T(8,128)(2,1)S(1)}, u32[]{:S(2)}, u32[]{:S(2)}) collective-permute-start(bf16[48,1024]{1,0:T(8,128)(2,1)S(1)} %get-tuple-element.17), channel_id=1, source_target_pairs={{0,6},{2,4},{4,2},{6,0},{1,7},{3,5},{5,3},{7,1},{8,14},{10,12},{12... | collective-permute-start | bytes 294920 | tf_op jit(solution)/shard_map/ppermute | solution.py:215
  25.0 5.5 %collective-permute-start.6 = (bf16[48,1024]{1,0:T(8,128)(2,1)S(1)}, bf16[48,1024]{1,0:T(8,128)(2,1)S(1)}, u32[]{:S(2)}, u32[]{:S(2)}) collective-permute-start(bf16[48,1024]{1,0:T(8,128)(2,1)S(1)} %get-tuple-element.15), channel_id=1, source_target_pairs={{0,2},{2,0},{4,6},{6,4},{1,3},{3,1},{5,7},{7,5},{8,10},{10,8},{12,... | collective-permute-start | bytes 294920 | tf_op jit(solution)/shard_map/ppermute | solution.py:215
  26.7 6.6 %collective-permute-start.7 = (bf16[48,1024]{1,0:T(8,128)(2,1)S(1)}, bf16[48,1024]{1,0:T(8,128)(2,1)S(1)}, u32[]{:S(2)}, u32[]{:S(2)}) collective-permute-start(bf16[48,1024]{1,0:T(8,128)(2,1)S(1)} %get-tuple-element.16), channel_id=1, source_target_pairs={{0,4},{2,6},{4,0},{6,2},{1,5},{3,7},{5,1},{7,3},{8,12},{10,14},{12... | collective-permute-start | bytes 294920 | tf_op jit(solution)/shard_map/ppermute | solution.py:215
  33.4 3.7 %collective-permute-start.9 = (bf16[32,1024]{1,0:T(8,128)(2,1)S(1)}, bf16[32,1024]{1,0:T(8,128)(2,1)S(1)}, u32[]{:S(2)}, u32[]{:S(2)}) collective-permute-start(bf16[32,1024]{1,0:T(8,128)(2,1)S(1)} %fusion.1), channel_id=1, source_target_pairs={{0,8},{8,16},{16,24},{24,0},{1,9},{9,17},{17,25},{25,1},{2,10},{10... | collective-permute-start | bytes 196616 | tf_op jit(solution)/shard_map/ppermute | solution.py:215
  33.4 4.5 %collective-permute-start.10 = (bf16[24,1024]{1,0:T(8,128)(2,1)S(1)}, bf16[24,1024]{1,0:T(8,128)(2,1)S(1)}, u32[]{:S(2)}, u32[]{:S(2)}) collective-permute-start(bf16[24,1024]{1,0:T(8,128)(2,1)S(1)} %get-tuple-element.19), channel_id=1, source_target_pairs={{0,9},{1,8},{8,17},{9,16},{16,25},{17,24},{24,1},{25,0},{2,11},{3,... | collective-permute-start | bytes 147464 | tf_op jit(solution)/shard_map/ppermute | solution.py:215

commit v2 on v1

--- a/solution.py
+++ b/solution.py
@@ -35,7 +35,19 @@
     return jnp.dot(left, right, preferred_element_type=f32)
 
 
-def pack_kernel(base_ref, stream_ref, gain_ref, probs_ref, ids_ref, meta_ref, *packed_refs, held_count):
+def pack_kernel(base_ref, stream_hbm, gain_hbm, probs_hbm, ids_hbm, meta_ref, *refs, held_count):
+    packed_refs = refs[:-5]
+    stream_ref, gain_ref, probs_ref, ids_ref, sems = refs[-5:]
+    copies = [
+        pltpu.make_async_copy(source, target, sems.at[index])
+        for index, (source, target) in enumerate(
+            ((ids_hbm, ids_ref), (probs_hbm, probs_ref), (stream_hbm, stream_ref), (gain_hbm, gain_ref))
+        )
+    ]
+    for copy in copies:
+        copy.start()
+    copies[0].wait()
+    copies[1].wait()
     ids = ids_ref[...]
     probs = probs_ref[...]
     weights = probs / jnp.sum(probs, axis=0, keepdims=True)
@@ -59,17 +71,6 @@
         [jnp.broadcast_to(position[e : e + 1], (GROUP, tokens)) for e in range(held_count)], axis=0
     )
     onehot = slot.astype(f32) == spread
-    packed = dot(jnp.where(onehot & left, 1.0, 0.0).astype(bf16), stream_ref[:, :half])
-    packed += dot(jnp.where(onehot & ~left, 1.0, 0.0).astype(bf16), stream_ref[:, half:])
-    squares = packed * packed
-    total = jnp.sum(squares + swap_halves(squares), axis=1, keepdims=True)
-    inverse_rms = lax.rsqrt(total / (2 * half) + epsilon)
-    gain = gain_ref[...].astype(f32)
-    left, _ = row_tables(rows, half)
-    normed = packed * inverse_rms * jnp.where(left, gain[:, :half], gain[:, half:])
-    per_ref = rows // len(packed_refs)
-    for index, ref in enumerate(packed_refs):
-        ref[...] = normed[index * per_ref : (index + 1) * per_ref].astype(bf16)
     lines = []
     for block in range(held_count):
         rest = coefficients[block]
@@ -78,23 +79,63 @@
             lines.append(piece)
             rest = rest - piece
         lines.append(position[block : block + 1])
-    table = jnp.concatenate(lines, axis=0)
-    meta_ref[...] = table.astype(bf16)
+    meta_ref[...] = jnp.concatenate(lines, axis=0).astype(bf16)
+    copies[2].wait()
+    packed = dot(jnp.where(onehot & left, 1.0, 0.0).astype(bf16), stream_ref[:, :half])
+    packed += dot(jnp.where(onehot & ~left, 1.0, 0.0).astype(bf16), stream_ref[:, half:])
+    squares = packed * packed
+    total = jnp.sum(squares + swap_halves(squares), axis=1, keepdims=True)
+    inverse_rms = lax.rsqrt(total / (2 * half) + epsilon)
+    copies[3].wait()
+    gain = gain_ref[...].astype(f32)
+    left, _ = row_tables(rows, half)
+    normed = packed * inverse_rms * jnp.where(left, gain[:, :half], gain[:, half:])
+    per_ref = rows // len(packed_refs)
+    for index, ref in enumerate(packed_refs):
+        ref[...] = normed[index * per_ref : (index + 1) * per_ref].astype(bf16)
 
 
 def pack(stream, gain, probs, ids, base, held_count, outputs):
     tokens, width = stream.shape
     rows = held_count * GROUP // outputs
     whole = pl.BlockSpec(memory_space=pltpu.VMEM)
+    far = pl.BlockSpec(memory_space=pltpu.HBM)
     return pl.pallas_call(
         functools.partial(pack_kernel, held_count=held_count),
         out_shape=[jax.ShapeDtypeStruct((4 * held_count, tokens), bf16)]
         + [jax.ShapeDtypeStruct((rows, width // 2), bf16)] * outputs,
-        in_specs=[pl.BlockSpec(memory_space=pltpu.SMEM)] + [whole] * 4,
+        in_specs=[pl.BlockSpec(memory_space=pltpu.SMEM)] + [far] * 4,
         out_specs=[whole] * (1 + outputs),
+        scratch_shapes=[pltpu.VMEM(array.shape, array.dtype) for array in (stream, gain, probs, ids)]
+        + [pltpu.SemaphoreType.DMA((4,))],
         compiler_params=pltpu.CompilerParams(vmem_limit_bytes=VMEM_LIMIT),
         cost_estimate=pl.CostEstimate(flops=2 * rows * tokens * width, bytes_accessed=2 * tokens * width, transcendentals=0),
-    )(base, stream, gain, probs, ids)
+    )(base, *[pltpu.with_memory_space_constraint(array, pltpu.HBM) for array in (stream, gain, probs, ids)])
+
+
+def load_kernel(gate_up_hbm, down_hbm, after_ref, gate_up_ref, down_ref, sems):
+    copies = [
+        pltpu.make_async_copy(gate_up_hbm, gate_up_ref, sems.at[0]),
+        pltpu.make_async_copy(down_hbm, down_ref, sems.at[1]),
+    ]
+    for copy in copies:
+        copy.start()
+    for copy in copies:
+        copy.wait()
+
+
+def load(gate_up, down, after):
+    whole = pl.BlockSpec(memory_space=pltpu.VMEM)
+    far = pl.BlockSpec(memory_space=pltpu.HBM)
+    return pl.pallas_call(
+        load_kernel,
+        out_shape=[jax.ShapeDtypeStruct(gate_up.shape, bf16), jax.ShapeDtypeStruct(down.shape, bf16)],
+        in_specs=[far, far, pl.BlockSpec(memory_space=pl.ANY)],
+        out_specs=[whole, whole],
+        scratch_shapes=[pltpu.SemaphoreType.DMA((2,))],
+        compiler_params=pltpu.CompilerParams(vmem_limit_bytes=VMEM_LIMIT),
+        cost_estimate=pl.CostEstimate(flops=0, bytes_accessed=2 * (gate_up.size + down.size), transcendentals=0),
+    )(*[pltpu.with_memory_space_constraint(array, pltpu.HBM) for array in (gate_up, down)], after)
 
 
 def expert_rows(value, gate_ref, up_ref, down_ref):
@@ -158,31 +199,34 @@
 
 
 def mix_kernel(meta_ref, *refs, held_count):
-    rows_refs, out_ref = refs[:-1], refs[-1]
-    half = out_ref.shape[1] // 2
-    tokens = out_ref.shape[0]
+    rows_refs, out_hbm, out_ref, sems = refs[:-3], refs[-3], refs[-2], refs[-1]
+    tokens, width = out_ref.shape
+    half = width // 2
     meta = meta_ref[:, :tokens].astype(f32)
-    left, slot = row_tables(GROUP, tokens)
-    blocks = []
-    for ref in rows_refs:
-        value = ref[...].astype(f32)
-        for first in range(0, value.shape[0] // GROUP * GROUP, GROUP):
-            blocks.append(value[first : first + GROUP])
-    values = jnp.concatenate(blocks[:held_count], axis=0).astype(bf16)
-    sides = [jnp.zeros((tokens, half), f32)] * 2
+    _, slot = row_tables(GROUP, tokens)
+    values = jnp.concatenate([ref[...].astype(f32) for ref in rows_refs], axis=0)
+    left, _ = row_tables(*values.shape)
+    sides = [jnp.where(left, values, 0.0).astype(bf16), jnp.where(left, 0.0, values).astype(bf16)]
+    held = [slot.astype(f32) == meta[4 * block + 3 : 4 * block + 4] for block in range(held_count)]
+    tables = []
     for piece in range(3):
-        tables = [[], []]
-        for block in range(held_count):
-            position = meta[4 * block + 3 : 4 * block + 4]
-            share = meta[4 * block + piece : 4 * block + piece + 1]
-            held = slot.astype(f32) == position
-            tables[0].append(jnp.where(held & left, share, 0.0))
-            tables[1].append(jnp.where(held & ~left, share, 0.0))
-        for side in range(2):
-            table = jnp.concatenate(tables[side], axis=0)
-            sides[side] = sides[side] + dot(table.T.astype(bf16), values)
-    out_ref[:, :half] = sides[0].astype(bf16)
-    out_ref[:, half:] = sides[1].astype(bf16)
+        table = jnp.concatenate(
+            [
+                jnp.where(held[block], meta[4 * block + piece : 4 * block + piece + 1], 0.0)
+                for block in range(held_count)
+            ],
+            axis=0,
+        )
+        tables.append(table.T.astype(bf16))
+    copies = []
+    for side in range(2):
+        columns = pl.ds(side * half, half)
+        total = sum(dot(table, sides[side]) for table in tables)
+        out_ref[:, columns] = total.astype(bf16)
+        copies.append(pltpu.make_async_copy(out_ref.at[:, columns], out_hbm.at[:, columns], sems.at[side]))
+        copies[side].start()
+    for copy in copies:
+        copy.wait()
 
 
 def mix(meta, blocks, tokens, held_count):
@@ -192,7 +236,8 @@
         functools.partial(mix_kernel, held_count=held_count),
         out_shape=jax.ShapeDtypeStruct((tokens, 2 * width), bf16),
         in_specs=[whole] * (1 + len(blocks)),
-        out_specs=whole,
+        out_specs=pl.BlockSpec(memory_space=pltpu.HBM),
+        scratch_shapes=[pltpu.VMEM((tokens, 2 * width), bf16), pltpu.SemaphoreType.DMA((2,))],
         compiler_params=pltpu.CompilerParams(vmem_limit_bytes=VMEM_LIMIT),
     )(meta, *blocks)
 
@@ -229,6 +274,7 @@
 def pair_shards(stream, gain, probs, ids, gate_up, down):
     base = lax.axis_index("expert").astype(jnp.int32).reshape(1)
     meta, own, other = pack(stream, gain, probs, ids, base, 2, 2)
+    gate_up, down = load(gate_up, down, own)
     other = move(other, ("expert",), lambda e: (e ^ 1,))
     own3, own2 = across(own, 3), across(own, 2)
     other3, other2 = across(other, 3), across(other, 2)

time: 39.9 us -> 35.1 us (0.88)
  local copies, waits for them, and re-layouts: 5.95 us -> 0.02 us
  Pallas kernels: 3.33 us -> 6.14 us
  waiting for transfers between devices: 10.7 us -> 8.16 us
  starting transfers between devices: 19.2 us -> 20.3 us
    unnamed x16 -> x0, local copies, waits for them, and re-layouts: 5.93 us -> none
    ppermute x11, waiting for transfers between devices: 10.7 us -> 8.16 us  [move(): return lax.ppermute(value, axes if len(axes) > 1 else axes[0], pairs)]
    pallas_call x0 -> x1, Pallas kernels: none -> 1.87 us  [load(): pl.pallas_call(load_kernel, out_shape=[jax.ShapeDtypeStruct(gate_up.shape...]
    ppermute x11, starting transfers between devices: 19.2 us -> 20.3 us  [move(): return lax.ppermute(value, axes if len(axes) > 1 else axes[0], pairs)]
    pallas_call x1, Pallas kernels: 0.44 us -> 1.45 us  [pack(): pl.pallas_call(functools.partial(pack_kernel, held_count=held_count), out...]
  transfers between devices with their start and end apart: 11 -> 11, of which waited for: 7 -> 5; matrix products, arithmetic and copies ran while one was open for 0% -> 0% of each run, Pallas kernels for 4% -> 10%
where the time goes in v2:
time: 35.1 us; the launch traced here: 34.8 us
  starting transfers between devices  20.3 us (58%)
  waiting for transfers between devices  8.16 us (23%)
  Pallas kernels  6.14 us (17%)
    ppermute x11, starting transfers between devices, move(): return lax.ppermute(value, axes if len(axes) > 1 else axes[0], pairs)  20.3 us
    ppermute x11, waiting for transfers between devices, move(): return lax.ppermute(value, axes if len(axes) > 1 else axes[0], pairs)  8.16 us
    pallas_call x1, Pallas kernels, load(): pl.pallas_call(load_kernel, out_shape=[jax.ShapeDtypeStruct(gate_up.shape...  1.87 us
    pallas_call x2, Pallas kernels, expert_quarter(): pl.pallas_call(functools.partial(expert_kernel, count=len(blocks)), out_s...  1.47 us
    pallas_call x1, Pallas kernels, pack(): pl.pallas_call(functools.partial(pack_kernel, held_count=held_count), out...  1.45 us
    pallas_call x1, Pallas kernels, mix(): pl.pallas_call(functools.partial(mix_kernel, held_count=held_count), out_...  1.35 us
  transfers between devices with their start and end apart: 11, of which 5 were waited for; matrix products, arithmetic and copies ran while one was open for 0% of the time, Pallas kernels for 10%

profile of v2, /device:TPU:0, one launch (start us, length us, event | category | flops | bytes accessed | tf_op | source)
XLA Modules:
  0.0 34.8 jit_solution(15725767833563774599)
XLA Ops:
  0.0 1.5 %shard_map.64 = (bf16[8,128]{1,0:T(8,128)(2,1)S(1)}, bf16[24,1024]{1,0:T(8,128)(2,1)S(1)}, bf16[24,1024]{1,0:T(8,128)(2,1)S(1)}) custom-call(s32[1]{0:T(128)} %bitcast.2.base_ref, bf16[128,2048]{1,0:T(8,128)(2,1)} %bitcast.13, bf16[1,2048]{1,0:T(2,128)(2,1)} %gain_hbm.1, f32[8,128]{1,0:T(8,128)} %bitcast.14, s32[8,128]{1,0:T(8,128)} %bitcast.15), custom_call_target="tpu_custom_call" | custom-call | flops 12582912 | bytes 524288 | tf_op jit(solution)/shard_map/pallas_call | solution.py:103
  1.5 3.0 %collective-permute-start = (bf16[24,1024]{1,0:T(8,128)(2,1)S(1)}, bf16[24,1024]{1,0:T(8,128)(2,1)S(1)}, u32[]{:S(2)}, u32[]{:S(2)}) collective-permute-start(bf16[24,1024]{1,0:T(8,128)(2,1)S(1)} %get-tuple-element.17), channel_id=1, source_target_pairs={{0,1},{1,0},{2,3},{3,2},{4,5},{5,4},{6,7},{7,6},{8,9},{9,8},{10,11... | collective-permute-start | bytes 147464 | tf_op jit(solution)/shard_map/ppermute | solution.py:260
  4.5 2.1 %collective-permute-done.refs_1_ = bf16[24,1024]{1,0:T(8,128)(2,1)S(1)} collective-permute-done((bf16[24,1024]{1,0:T(8,128)(2,1)S(1)}, bf16[24,1024]{1,0:T(8,128)(2,1)S(1)}, u32[]{:S(2)}, u32[]{:S(2)}) %collective-permute-start) | collective-permute-done | bytes 49184 | tf_op jit(solution)/shard_map/ppermute | solution.py:260
  6.5 2.2 %collective-permute-start.5 = (bf16[48,1024]{1,0:T(8,128)(2,1)S(1)}, bf16[48,1024]{1,0:T(8,128)(2,1)S(1)}, u32[]{:S(2)}, u32[]{:S(2)}) collective-permute-start(bf16[48,1024]{1,0:T(8,128)(2,1)S(1)} %pad_maximum_fusion), channel_id=1, source_target_pairs={{0,2},{2,0},{4,6},{6,4},{1,3},{3,1},{5,7},{7,5},{8,10},{10,8},{12,... | collective-permute-start | bytes 294920 | tf_op jit(solution)/shard_map/ppermute | solution.py:260
  8.7 2.5 %collective-permute-start.1 = (bf16[24,1024]{1,0:T(8,128)(2,1)S(1)}, bf16[24,1024]{1,0:T(8,128)(2,1)S(1)}, u32[]{:S(2)}, u32[]{:S(2)}) collective-permute-start(bf16[24,1024]{1,0:T(8,128)(2,1)S(1)} %get-tuple-element.14.after_ref.refs_0_), channel_id=1, source_target_pairs={{0,6},{2,4},{4,2},{6,0},{1,7},{3,5},{5,3},{7,1},{8,14},{10,12},{12... | collective-permute-start | bytes 147464 | tf_op jit(solution)/shard_map/ppermute | solution.py:260
  11.2 1.3 %collective-permute-start.2 = (bf16[24,1024]{1,0:T(8,128)(2,1)S(1)}, bf16[24,1024]{1,0:T(8,128)(2,1)S(1)}, u32[]{:S(2)}, u32[]{:S(2)}) collective-permute-start(bf16[24,1024]{1,0:T(8,128)(2,1)S(1)} %collective-permute-done.refs_1_), channel_id=1, source_target_pairs={{0,6},{2,4},{4,2},{6,0},{1,7},{3,5},{5,3},{7,1},{8,14},{10,12},{12... | collective-permute-start | bytes 147464 | tf_op jit(solution)/shard_map/ppermute | solution.py:260
  12.5 0.8 %collective-permute-start.3 = (bf16[24,1024]{1,0:T(8,128)(2,1)S(1)}, bf16[24,1024]{1,0:T(8,128)(2,1)S(1)}, u32[]{:S(2)}, u32[]{:S(2)}) collective-permute-start(bf16[24,1024]{1,0:T(8,128)(2,1)S(1)} %get-tuple-element.14.after_ref.refs_0_), channel_id=1, source_target_pairs={{0,4},{2,6},{4,0},{6,2},{1,5},{3,7},{5,1},{7,3},{8,12},{10,14},{12... | collective-permute-start | bytes 147464 | tf_op jit(solution)/shard_map/ppermute | solution.py:260
  13.3 2.1 %collective-permute-start.4 = (bf16[24,1024]{1,0:T(8,128)(2,1)S(1)}, bf16[24,1024]{1,0:T(8,128)(2,1)S(1)}, u32[]{:S(2)}, u32[]{:S(2)}) collective-permute-start(bf16[24,1024]{1,0:T(8,128)(2,1)S(1)} %collective-permute-done.refs_1_), channel_id=1, source_target_pairs={{0,4},{2,6},{4,0},{6,2},{1,5},{3,7},{5,1},{7,3},{8,12},{10,14},{12... | collective-permute-start | bytes 147464 | tf_op jit(solution)/shard_map/ppermute | solution.py:260
  15.5 1.9 %shard_map.65 = (bf16[2,2048,256]{2,1,0:T(8,128)(2,1)S(1)}, bf16[256,2048]{1,0:T(8,128)(2,1)S(1)}) custom-call(bf16[2,2048,256]{2,1,0:T(8,128)(2,1)} %bitcast.11, bf16[256,2048]{1,0:T(8,128)(2,1)} %bitcast.12, bf16[24,1024]{1,0:T(8,128)(2,1)S(1)} %get-tuple-element.14.after_ref.refs_0_), custom_call_target="tpu_custom_call" | custom-call | bytes 3145728 | tf_op jit(solution)/shard_map/pallas_call | solution.py:130
  17.3 0.0 collective-permute-done.1.refs_2_
  17.4 0.0 collective-permute-done.2.refs_3_
  17.4 0.7 %shard_map.66 = (bf16[48,1024]{1,0:T(8,128)(2,1)S(1)}, bf16[48,1024]{1,0:T(8,128)(2,1)S(1)}) custom-call(bf16[2,2048,256]{2,1,0:T(8,128)(2,1)S(1)} %get-tuple-element.15.gate_up_ref, bf16[256,2048]{1,0:T(8,128)(2,1)S(1)} %get-tuple-element.16.down_ref, bf16[24,1024]{1,0:T(8,128)(2,1)S(1)} %get-tuple-element.14.after_ref.refs_0_, ...), custom_call_target="tpu_custom_call" | custom-call | flops 150994944 | bytes 3145728 | tf_op jit(solution)/shard_map/pallas_call | solution.py:168
  18.1 2.5 %collective-permute-start.8 = (bf16[48,1024]{1,0:T(8,128)(2,1)S(1)}, bf16[48,1024]{1,0:T(8,128)(2,1)S(1)}, u32[]{:S(2)}, u32[]{:S(2)}) collective-permute-start(bf16[48,1024]{1,0:T(8,128)(2,1)S(1)} %get-tuple-element.21), channel_id=1, source_target_pairs={{0,6},{2,4},{4,2},{6,0},{1,7},{3,5},{5,3},{7,1},{8,14},{10,12},{12... | collective-permute-start | bytes 294920 | tf_op jit(solution)/shard_map/ppermute | solution.py:260
  20.6 0.0 collective-permute-done.3.refs_0_
  20.7 1.1 %collective-permute-done.4.refs_1_ = bf16[24,1024]{1,0:T(8,128)(2,1)S(1)} collective-permute-done((bf16[24,1024]{1,0:T(8,128)(2,1)S(1)}, bf16[24,1024]{1,0:T(8,128)(2,1)S(1)}, u32[]{:S(2)}, u32[]{:S(2)}) %collective-permute-start.4) | collective-permute-done | bytes 49184 | tf_op jit(solution)/shard_map/ppermute | solution.py:260
  21.8 0.0 collective-permute-done.5.refs_2_
  21.8 0.7 %shard_map.67 = (bf16[48,1024]{1,0:T(8,128)(2,1)S(1)}, bf16[48,1024]{1,0:T(8,128)(2,1)S(1)}) custom-call(bf16[2,2048,256]{2,1,0:T(8,128)(2,1)S(1)} %get-tuple-element.15.gate_up_ref, bf16[256,2048]{1,0:T(8,128)(2,1)S(1)} %get-tuple-element.16.down_ref, bf16[24,1024]{1,0:T(8,128)(2,1)S(1)} %collective-permute-done.3.refs_0_, ...), custom_call_target="tpu_custom_call" | custom-call | flops 150994944 | bytes 3145728 | tf_op jit(solution)/shard_map/pallas_call | solution.py:168
  22.5 0.1 collective-permute-start.6
  22.6 3.0 %collective-permute-start.7 = (bf16[48,1024]{1,0:T(8,128)(2,1)S(1)}, bf16[48,1024]{1,0:T(8,128)(2,1)S(1)}, u32[]{:S(2)}, u32[]{:S(2)}) collective-permute-start(bf16[48,1024]{1,0:T(8,128)(2,1)S(1)} %get-tuple-element.20), channel_id=1, source_target_pairs={{0,4},{2,6},{4,0},{6,2},{1,5},{3,7},{5,1},{7,3},{8,12},{10,14},{12... | collective-permute-start | bytes 294920 | tf_op jit(solution)/shard_map/ppermute | solution.py:260
  25.6 0.0 collective-permute-done.8
  25.6 3.2 %collective-permute-done.6 = bf16[48,1024]{1,0:T(8,128)(2,1)S(1)} collective-permute-done((bf16[48,1024]{1,0:T(8,128)(2,1)S(1)}, bf16[48,1024]{1,0:T(8,128)(2,1)S(1)}, u32[]{:S(2)}, u32[]{:S(2)}) %collective-permute-start.6) | collective-permute-done | bytes 98336 | tf_op jit(solution)/shard_map/ppermute | solution.py:260
  28.8 0.0 collective-permute-done.7
  28.8 0.1 add_convert_fusion
  28.9 0.1 collective-permute-start.9
  28.9 2.7 %collective-permute-start.10 = (bf16[24,1024]{1,0:T(8,128)(2,1)S(1)}, bf16[24,1024]{1,0:T(8,128)(2,1)S(1)}, u32[]{:S(2)}, u32[]{:S(2)}) collective-permute-start(bf16[24,1024]{1,0:T(8,128)(2,1)S(1)} %get-tuple-element.23), channel_id=1, source_target_pairs={{0,9},{1,8},{8,17},{9,16},{16,25},{17,24},{24,1},{25,0},{2,11},{3,... | collective-permute-start | bytes 147464 | tf_op jit(solution)/shard_map/ppermute | solution.py:260
  31.7 1.0 %collective-permute-done.9 = bf16[32,1024]{1,0:T(8,128)(2,1)S(1)} collective-permute-done((bf16[32,1024]{1,0:T(8,128)(2,1)S(1)}, bf16[32,1024]{1,0:T(8,128)(2,1)S(1)}, u32[]{:S(2)}, u32[]{:S(2)}) %collective-permute-start.9) | collective-permute-done | bytes 65568 | tf_op jit(solution)/shard_map/ppermute | solution.py:260
  32.6 0.8 %collective-permute-done.10.refs_1_ = bf16[24,1024]{1,0:T(8,128)(2,1)S(1)} collective-permute-done((bf16[24,1024]{1,0:T(8,128)(2,1)S(1)}, bf16[24,1024]{1,0:T(8,128)(2,1)S(1)}, u32[]{:S(2)}, u32[]{:S(2)}) %collective-permute-start.10) | collective-permute-done | bytes 49184 | tf_op jit(solution)/shard_map/ppermute | solution.py:260
  33.4 1.3 %shard_map.68 = bf16[128,2048]{1,0:T(8,128)(2,1)} custom-call(bf16[8,1024]{1,0:T(8,128)(2,1)S(1)} %slice.17.meta_ref, bf16[24,1024]{1,0:T(8,128)(2,1)S(1)} %slice.18.refs_0_, bf16[24,1024]{1,0:T(8,128)(2,1)S(1)} %collective-permute-done.10.refs_1_), custom_call_target="tpu_custom_call" | custom-call | tf_op jit(solution)/shard_map/pallas_call | solution.py:235
  (5 shorter events, 0.0 us)
Async XLA Ops:
  1.5 5.1 %collective-permute-start = (bf16[24,1024]{1,0:T(8,128)(2,1)S(1)}, bf16[24,1024]{1,0:T(8,128)(2,1)S(1)}, u32[]{:S(2)}, u32[]{:S(2)}) collective-permute-start(bf16[24,1024]{1,0:T(8,128)(2,1)S(1)} %get-tuple-element.17), channel_id=1, source_target_pairs={{0,1},{1,0},{2,3},{3,2},{4,5},{5,4},{6,7},{7,6},{8,9},{9,8},{10,11... | collective-permute-start | bytes 147464 | tf_op jit(solution)/shard_map/ppermute | solution.py:260
  6.5 15.2 %collective-permute-start.5 = (bf16[48,1024]{1,0:T(8,128)(2,1)S(1)}, bf16[48,1024]{1,0:T(8,128)(2,1)S(1)}, u32[]{:S(2)}, u32[]{:S(2)}) collective-permute-start(bf16[48,1024]{1,0:T(8,128)(2,1)S(1)} %pad_maximum_fusion), channel_id=1, source_target_pairs={{0,2},{2,0},{4,6},{6,4},{1,3},{3,1},{5,7},{7,5},{8,10},{10,8},{12,... | collective-permute-start | bytes 294920 | tf_op jit(solution)/shard_map/ppermute | solution.py:260
  8.7 8.6 %collective-permute-start.1 = (bf16[24,1024]{1,0:T(8,128)(2,1)S(1)}, bf16[24,1024]{1,0:T(8,128)(2,1)S(1)}, u32[]{:S(2)}, u32[]{:S(2)}) collective-permute-start(bf16[24,1024]{1,0:T(8,128)(2,1)S(1)} %get-tuple-element.14.after_ref.refs_0_), channel_id=1, source_target_pairs={{0,6},{2,4},{4,2},{6,0},{1,7},{3,5},{5,3},{7,1},{8,14},{10,12},{12... | collective-permute-start | bytes 147464 | tf_op jit(solution)/shard_map/ppermute | solution.py:260
  11.2 6.2 %collective-permute-start.2 = (bf16[24,1024]{1,0:T(8,128)(2,1)S(1)}, bf16[24,1024]{1,0:T(8,128)(2,1)S(1)}, u32[]{:S(2)}, u32[]{:S(2)}) collective-permute-start(bf16[24,1024]{1,0:T(8,128)(2,1)S(1)} %collective-permute-done.refs_1_), channel_id=1, source_target_pairs={{0,6},{2,4},{4,2},{6,0},{1,7},{3,5},{5,3},{7,1},{8,14},{10,12},{12... | collective-permute-start | bytes 147464 | tf_op jit(solution)/shard_map/ppermute | solution.py:260
  12.5 8.1 %collective-permute-start.3 = (bf16[24,1024]{1,0:T(8,128)(2,1)S(1)}, bf16[24,1024]{1,0:T(8,128)(2,1)S(1)}, u32[]{:S(2)}, u32[]{:S(2)}) collective-permute-start(bf16[24,1024]{1,0:T(8,128)(2,1)S(1)} %get-tuple-element.14.after_ref.refs_0_), channel_id=1, source_target_pairs={{0,4},{2,6},{4,0},{6,2},{1,5},{3,7},{5,1},{7,3},{8,12},{10,14},{12... | collective-permute-start | bytes 147464 | tf_op jit(solution)/shard_map/ppermute | solution.py:260
  13.3 8.4 %collective-permute-start.4 = (bf16[24,1024]{1,0:T(8,128)(2,1)S(1)}, bf16[24,1024]{1,0:T(8,128)(2,1)S(1)}, u32[]{:S(2)}, u32[]{:S(2)}) collective-permute-start(bf16[24,1024]{1,0:T(8,128)(2,1)S(1)} %collective-permute-done.refs_1_), channel_id=1, source_target_pairs={{0,4},{2,6},{4,0},{6,2},{1,5},{3,7},{5,1},{7,3},{8,12},{10,14},{12... | collective-permute-start | bytes 147464 | tf_op jit(solution)/shard_map/ppermute | solution.py:260
  18.1 7.4 %collective-permute-start.8 = (bf16[48,1024]{1,0:T(8,128)(2,1)S(1)}, bf16[48,1024]{1,0:T(8,128)(2,1)S(1)}, u32[]{:S(2)}, u32[]{:S(2)}) collective-permute-start(bf16[48,1024]{1,0:T(8,128)(2,1)S(1)} %get-tuple-element.21), channel_id=1, source_target_pairs={{0,6},{2,4},{4,2},{6,0},{1,7},{3,5},{5,3},{7,1},{8,14},{10,12},{12... | collective-permute-start | bytes 294920 | tf_op jit(solution)/shard_map/ppermute | solution.py:260
  22.5 6.3 %collective-permute-start.6 = (bf16[48,1024]{1,0:T(8,128)(2,1)S(1)}, bf16[48,1024]{1,0:T(8,128)(2,1)S(1)}, u32[]{:S(2)}, u32[]{:S(2)}) collective-permute-start(bf16[48,1024]{1,0:T(8,128)(2,1)S(1)} %get-tuple-element.19), channel_id=1, source_target_pairs={{0,2},{2,0},{4,6},{6,4},{1,3},{3,1},{5,7},{7,5},{8,10},{10,8},{12,... | collective-permute-start | bytes 294920 | tf_op jit(solution)/shard_map/ppermute | solution.py:260
  22.6 6.2 %collective-permute-start.7 = (bf16[48,1024]{1,0:T(8,128)(2,1)S(1)}, bf16[48,1024]{1,0:T(8,128)(2,1)S(1)}, u32[]{:S(2)}, u32[]{:S(2)}) collective-permute-start(bf16[48,1024]{1,0:T(8,128)(2,1)S(1)} %get-tuple-element.20), channel_id=1, source_target_pairs={{0,4},{2,6},{4,0},{6,2},{1,5},{3,7},{5,1},{7,3},{8,12},{10,14},{12... | collective-permute-start | bytes 294920 | tf_op jit(solution)/shard_map/ppermute | solution.py:260
  28.9 3.7 %collective-permute-start.9 = (bf16[32,1024]{1,0:T(8,128)(2,1)S(1)}, bf16[32,1024]{1,0:T(8,128)(2,1)S(1)}, u32[]{:S(2)}, u32[]{:S(2)}) collective-permute-start(bf16[32,1024]{1,0:T(8,128)(2,1)S(1)} %fusion.1), channel_id=1, source_target_pairs={{0,8},{8,16},{16,24},{24,0},{1,9},{9,17},{17,25},{25,1},{2,10},{10... | collective-permute-start | bytes 196616 | tf_op jit(solution)/shard_map/ppermute | solution.py:260
  28.9 4.5 %collective-permute-start.10 = (bf16[24,1024]{1,0:T(8,128)(2,1)S(1)}, bf16[24,1024]{1,0:T(8,128)(2,1)S(1)}, u32[]{:S(2)}, u32[]{:S(2)}) collective-permute-start(bf16[24,1024]{1,0:T(8,128)(2,1)S(1)} %get-tuple-element.23), channel_id=1, source_target_pairs={{0,9},{1,8},{8,17},{9,16},{16,25},{17,24},{24,1},{25,0},{2,11},{3,... | collective-permute-start | bytes 147464 | tf_op jit(solution)/shard_map/ppermute | solution.py:260

commit v3 on v2

--- a/solution.py
+++ b/solution.py
@@ -12,6 +12,8 @@
 epsilon = 1e-06
 f32 = jnp.float32
 bf16 = jnp.bfloat16
+LOAD_PIECES = 2
+MIX_PIECES = 2
 VMEM_LIMIT = 40 * 1024 * 1024
 
 
@@ -35,14 +37,22 @@
     return jnp.dot(left, right, preferred_element_type=f32)
 
 
-def pack_kernel(base_ref, stream_hbm, gain_hbm, probs_hbm, ids_hbm, meta_ref, *refs, held_count):
-    packed_refs = refs[:-5]
-    stream_ref, gain_ref, probs_ref, ids_ref, sems = refs[-5:]
+def pack_kernel(base_ref, ids_hbm, probs_hbm, stream_hbm, gain_hbm, gate_up_hbm, down_hbm, meta_ref, *refs, held_count):
+    packed_refs = refs[:-7]
+    gate_up_ref, down_ref = refs[-7:-5]
+    ids_ref, probs_ref, stream_ref, gain_ref, sems = refs[-5:]
+    pairs = [(ids_hbm, ids_ref), (probs_hbm, probs_ref), (stream_hbm, stream_ref), (gain_hbm, gain_ref)]
+    depth = gate_up_ref.shape[1] // LOAD_PIECES
+    for matrix in range(2):
+        for piece in range(LOAD_PIECES):
+            place = (matrix, pl.ds(piece * depth, depth))
+            pairs.append((gate_up_hbm.at[place], gate_up_ref.at[place]))
+    depth = down_ref.shape[0] // LOAD_PIECES
+    for piece in range(LOAD_PIECES):
+        place = pl.ds(piece * depth, depth)
+        pairs.append((down_hbm.at[place], down_ref.at[place]))
     copies = [
-        pltpu.make_async_copy(source, target, sems.at[index])
-        for index, (source, target) in enumerate(
-            ((ids_hbm, ids_ref), (probs_hbm, probs_ref), (stream_hbm, stream_ref), (gain_hbm, gain_ref))
-        )
+        pltpu.make_async_copy(source, target, sems.at[index]) for index, (source, target) in enumerate(pairs)
     ]
     for copy in copies:
         copy.start()
@@ -93,49 +103,27 @@
     per_ref = rows // len(packed_refs)
     for index, ref in enumerate(packed_refs):
         ref[...] = normed[index * per_ref : (index + 1) * per_ref].astype(bf16)
-
-
-def pack(stream, gain, probs, ids, base, held_count, outputs):
+    for copy in copies[4:]:
+        copy.wait()
+
+
+def pack(stream, gain, probs, ids, gate_up, down, base, held_count, outputs):
     tokens, width = stream.shape
     rows = held_count * GROUP // outputs
     whole = pl.BlockSpec(memory_space=pltpu.VMEM)
     far = pl.BlockSpec(memory_space=pltpu.HBM)
+    arrays = (ids, probs, stream, gain, gate_up, down)
     return pl.pallas_call(
         functools.partial(pack_kernel, held_count=held_count),
         out_shape=[jax.ShapeDtypeStruct((4 * held_count, tokens), bf16)]
-        + [jax.ShapeDtypeStruct((rows, width // 2), bf16)] * outputs,
-        in_specs=[pl.BlockSpec(memory_space=pltpu.SMEM)] + [far] * 4,
-        out_specs=[whole] * (1 + outputs),
-        scratch_shapes=[pltpu.VMEM(array.shape, array.dtype) for array in (stream, gain, probs, ids)]
-        + [pltpu.SemaphoreType.DMA((4,))],
-        compiler_params=pltpu.CompilerParams(vmem_limit_bytes=VMEM_LIMIT),
-        cost_estimate=pl.CostEstimate(flops=2 * rows * tokens * width, bytes_accessed=2 * tokens * width, transcendentals=0),
-    )(base, *[pltpu.with_memory_space_constraint(array, pltpu.HBM) for array in (stream, gain, probs, ids)])
-
-
-def load_kernel(gate_up_hbm, down_hbm, after_ref, gate_up_ref, down_ref, sems):
-    copies = [
-        pltpu.make_async_copy(gate_up_hbm, gate_up_ref, sems.at[0]),
-        pltpu.make_async_copy(down_hbm, down_ref, sems.at[1]),
-    ]
-    for copy in copies:
-        copy.start()
-    for copy in copies:
-        copy.wait()
-
-
-def load(gate_up, down, after):
-    whole = pl.BlockSpec(memory_space=pltpu.VMEM)
-    far = pl.BlockSpec(memory_space=pltpu.HBM)
-    return pl.pallas_call(
-        load_kernel,
-        out_shape=[jax.ShapeDtypeStruct(gate_up.shape, bf16), jax.ShapeDtypeStruct(down.shape, bf16)],
-        in_specs=[far, far, pl.BlockSpec(memory_space=pl.ANY)],
-        out_specs=[whole, whole],
-        scratch_shapes=[pltpu.SemaphoreType.DMA((2,))],
-        compiler_params=pltpu.CompilerParams(vmem_limit_bytes=VMEM_LIMIT),
-        cost_estimate=pl.CostEstimate(flops=0, bytes_accessed=2 * (gate_up.size + down.size), transcendentals=0),
-    )(*[pltpu.with_memory_space_constraint(array, pltpu.HBM) for array in (gate_up, down)], after)
+        + [jax.ShapeDtypeStruct((rows, width // 2), bf16)] * outputs
+        + [jax.ShapeDtypeStruct(gate_up.shape, bf16), jax.ShapeDtypeStruct(down.shape, bf16)],
+        in_specs=[pl.BlockSpec(memory_space=pltpu.SMEM)] + [far] * len(arrays),
+        out_specs=[whole] * (3 + outputs),
+        scratch_shapes=[pltpu.VMEM(array.shape, array.dtype) for array in arrays[:4]]
+        + [pltpu.SemaphoreType.DMA((4 + 3 * LOAD_PIECES,))],
+        compiler_params=pltpu.CompilerParams(vmem_limit_bytes=VMEM_LIMIT),
+    )(base, *[pltpu.with_memory_space_constraint(array, pltpu.HBM) for array in arrays])
 
 
 def expert_rows(value, gate_ref, up_ref, down_ref):
@@ -163,7 +151,6 @@
 
 def expert_quarter(blocks, out_rows, gate_up, down):
     width = blocks[0].shape[1]
-    rows = sum(block.shape[0] for block in blocks)
     whole = pl.BlockSpec(memory_space=pltpu.VMEM)
     return pl.pallas_call(
         functools.partial(expert_kernel, count=len(blocks)),
@@ -171,9 +158,6 @@
         in_specs=[whole] * (2 + len(blocks)),
         out_specs=[whole] * len(out_rows),
         compiler_params=pltpu.CompilerParams(vmem_limit_bytes=VMEM_LIMIT),
-        cost_estimate=pl.CostEstimate(
-            flops=rows * 3 * down.size, bytes_accessed=2 * (gate_up.size + down.size), transcendentals=rows * down.shape[0]
-        ),
     )(gate_up, down, *blocks)
 
 
@@ -198,48 +182,62 @@
     )(gate_up, down, block)
 
 
-def mix_kernel(meta_ref, *refs, held_count):
-    rows_refs, out_hbm, out_ref, sems = refs[:-3], refs[-3], refs[-2], refs[-1]
-    tokens, width = out_ref.shape
-    half = width // 2
+def table_kernel(meta_ref, table_ref, *, held_count):
+    tokens = table_ref.shape[0]
     meta = meta_ref[:, :tokens].astype(f32)
     _, slot = row_tables(GROUP, tokens)
+    lines = []
+    for piece in range(3):
+        for block in range(held_count):
+            position = meta[4 * block + 3 : 4 * block + 4]
+            share = meta[4 * block + piece : 4 * block + piece + 1]
+            lines.append(jnp.where(slot.astype(f32) == position, share, 0.0))
+    table_ref[...] = jnp.concatenate(lines, axis=0).T.astype(bf16)
+
+
+def share_table(meta, tokens, held_count):
+    whole = pl.BlockSpec(memory_space=pltpu.VMEM)
+    return pl.pallas_call(
+        functools.partial(table_kernel, held_count=held_count),
+        out_shape=jax.ShapeDtypeStruct((tokens, 3 * GROUP * held_count), bf16),
+        in_specs=[whole],
+        out_specs=whole,
+        compiler_params=pltpu.CompilerParams(vmem_limit_bytes=VMEM_LIMIT),
+    )(meta)
+
+
+def mix_kernel(table_ref, *refs):
+    rows_refs, out_hbm, out_ref, sems = refs[:-3], refs[-3], refs[-2], refs[-1]
+    half = out_ref.shape[1] // 2
     values = jnp.concatenate([ref[...].astype(f32) for ref in rows_refs], axis=0)
     left, _ = row_tables(*values.shape)
     sides = [jnp.where(left, values, 0.0).astype(bf16), jnp.where(left, 0.0, values).astype(bf16)]
-    held = [slot.astype(f32) == meta[4 * block + 3 : 4 * block + 4] for block in range(held_count)]
-    tables = []
-    for piece in range(3):
-        table = jnp.concatenate(
-            [
-                jnp.where(held[block], meta[4 * block + piece : 4 * block + piece + 1], 0.0)
-                for block in range(held_count)
-            ],
-            axis=0,
-        )
-        tables.append(table.T.astype(bf16))
     copies = []
-    for side in range(2):
-        columns = pl.ds(side * half, half)
-        total = sum(dot(table, sides[side]) for table in tables)
+    for step in range(2 * MIX_PIECES):
+        side, piece = divmod(step, MIX_PIECES)
+        length = half // MIX_PIECES
+        columns = pl.ds(step * length, length)
+        value = sides[side][:, piece * length : (piece + 1) * length]
+        total = dot(table_ref[...], jnp.concatenate([value] * 3, axis=0))
         out_ref[:, columns] = total.astype(bf16)
-        copies.append(pltpu.make_async_copy(out_ref.at[:, columns], out_hbm.at[:, columns], sems.at[side]))
-        copies[side].start()
+        copies.append(pltpu.make_async_copy(out_ref.at[:, columns], out_hbm.at[:, columns], sems.at[step]))
+        copies[step].start()
     for copy in copies:
         copy.wait()
 
 
-def mix(meta, blocks, tokens, held_count):
+def mix(table, blocks):
+    tokens = table.shape[0]
     width = blocks[0].shape[1]
     whole = pl.BlockSpec(memory_space=pltpu.VMEM)
     return pl.pallas_call(
-        functools.partial(mix_kernel, held_count=held_count),
+        mix_kernel,
         out_shape=jax.ShapeDtypeStruct((tokens, 2 * width), bf16),
         in_specs=[whole] * (1 + len(blocks)),
         out_specs=pl.BlockSpec(memory_space=pltpu.HBM),
-        scratch_shapes=[pltpu.VMEM((tokens, 2 * width), bf16), pltpu.SemaphoreType.DMA((2,))],
-        compiler_params=pltpu.CompilerParams(vmem_limit_bytes=VMEM_LIMIT),
-    )(meta, *blocks)
+        scratch_shapes=[pltpu.VMEM((tokens, 2 * width), bf16), pltpu.SemaphoreType.DMA((2 * MIX_PIECES,))],
+        compiler_params=pltpu.CompilerParams(vmem_limit_bytes=VMEM_LIMIT),
+    )(table, *blocks)
 
 
 def move(value, axes, target):
@@ -273,30 +271,31 @@
 
 def pair_shards(stream, gain, probs, ids, gate_up, down):
     base = lax.axis_index("expert").astype(jnp.int32).reshape(1)
-    meta, own, other = pack(stream, gain, probs, ids, base, 2, 2)
-    gate_up, down = load(gate_up, down, own)
+    meta, own, other, gate_up, down = pack(stream, gain, probs, ids, gate_up, down, base, 2, 2)
     other = move(other, ("expert",), lambda e: (e ^ 1,))
-    own3, own2 = across(own, 3), across(own, 2)
-    other3, other2 = across(other, 3), across(other, 2)
-    both1 = across(jnp.concatenate([own, other], axis=0), 1)
-    part0, part3 = expert_quarter([own, other, own3, other3], [2 * GROUP] * 2, gate_up, down)
-    back3 = across(part3, 3)
-    part2, part1 = expert_quarter([own2, other2, both1], [2 * GROUP] * 2, gate_up, down)
-    back2, back1 = across(part2, 2), across(part1, 1)
-    summed = added([part0, back1, back2, back3])
-    tagged = jnp.concatenate(
-        [summed[:GROUP], jnp.pad(meta, ((0, 0), (0, summed.shape[1] - meta.shape[1])))], axis=0
-    )
+    blocks = {0: [own, other]}
+    for step in (3, 2, 1):
+        blocks[step] = [across(own, step), across(other, step)]
+    rows = 2 * GROUP
+    part0, part1 = expert_quarter(blocks[0] + blocks[1], [rows, rows], gate_up, down)
+    back2 = across(expert_quarter(blocks[2], [rows], gate_up, down)[0], 2)
+    back3 = across(expert_quarter(blocks[3], [rows], gate_up, down)[0], 3)
+    direct = move(part1[:GROUP], ("section", "dp"), lambda s, q: (s + 1, q ^ 1))
+    direct_crossed = move(part1[GROUP:], ("section", "dp", "expert"), lambda s, q, e: (s + 1, q ^ 1, e ^ 1))
+    summed = added([part0, back2, back3])
+    wide = jnp.pad(meta, ((0, 0), (0, summed.shape[1] - meta.shape[1])))
+    tagged = jnp.concatenate([summed[:GROUP], wide], axis=0)
     tagged = move(tagged, ("section",), lambda s: (s + 1,))
     crossed = move(summed[GROUP:], ("section", "expert"), lambda s, e: (s + 1, e ^ 1))
-    return mix(tagged[GROUP:], [tagged[:GROUP], crossed], stream.shape[0], 2)
+    table = share_table(tagged[GROUP:], stream.shape[0], 2)
+    return mix(table, [added([tagged[:GROUP], direct]), added([crossed, direct_crossed])])
 
 
 def many_shards(stream, gain, probs, ids, gate_up, down):
     held_count = lax.axis_size("expert")
     group_count = lax.axis_size("dp")
     base = jnp.zeros((1,), jnp.int32)
-    meta, packed = pack(stream, gain, probs, ids, base, held_count, 1)
+    meta, packed, gate_up, down = pack(stream, gain, probs, ids, gate_up, down, base, held_count, 1)
     meta = move(meta, ("section",), lambda s: (s + 1,))
     shape = packed.shape
     split = (held_count, GROUP, shape[1])
@@ -312,7 +311,7 @@
     for step in range(1, group_count):
         parts.append(shifted(expert_quarter_many(shifted(received, step), gate_up, down), -step))
     summed = move(exchanged(added(parts)), ("section",), lambda s: (s + 1,))
-    return mix(meta, [summed], stream.shape[0], held_count)
+    return mix(share_table(meta, stream.shape[0], held_count), [summed])
 
 
 def shards(stream, norm_gain, gate_probs, expert_ids, gate_up_weight, down_weight):

time: 35.1 us -> 31.8 us (0.906)
  waiting for transfers between devices: 8.16 us -> 2.66 us
  starting transfers between devices: 20.3 us -> 23.3 us
  Pallas kernels: 6.14 us -> 5.47 us
    ppermute x11 -> x13, waiting for transfers between devices: 8.16 us -> 2.66 us  [move(): return lax.ppermute(value, axes if len(axes) > 1 else axes[0], pairs)]
    ppermute x11 -> x13, starting transfers between devices: 20.3 us -> 23.3 us  [move(): return lax.ppermute(value, axes if len(axes) > 1 else axes[0], pairs)]
    pallas_call x2, Pallas kernels: 3.22 us -> 1.13 us  [the longest x1 1.02 us: mix(): pl.pallas_call(mix_kernel, out_shape=jax.ShapeDtypeStruct((tokens, 2 * wi...]
    pallas_call x2 -> x3, Pallas kernels: 1.47 us -> 2.22 us  [expert_quarter(): pl.pallas_call(functools.partial(expert_kernel, count=len(blocks)), out_s...]
    pallas_call x1, Pallas kernels: 1.45 us -> 2.12 us  [pack(): pl.pallas_call(functools.partial(pack_kernel, held_count=held_count), out...]
  transfers between devices with their start and end apart: 11 -> 13, of which waited for: 5 -> 2; matrix products, arithmetic and copies ran while one was open for 0% -> 0% of each run, Pallas kernels for 10% -> 7%
where the time goes in v3:
time: 31.8 us; the launch traced here: 31.6 us
  starting transfers between devices  23.3 us (73%)
  Pallas kernels  5.47 us (17%)
  waiting for transfers between devices  2.66 us (8%)
    ppermute x13, starting transfers between devices, move(): return lax.ppermute(value, axes if len(axes) > 1 else axes[0], pairs)  23.3 us
    ppermute x13, waiting for transfers between devices, move(): return lax.ppermute(value, axes if len(axes) > 1 else axes[0], pairs)  2.66 us
    pallas_call x3, Pallas kernels, expert_quarter(): pl.pallas_call(functools.partial(expert_kernel, count=len(blocks)), out_s...  2.22 us
    pallas_call x1, Pallas kernels, pack(): pl.pallas_call(functools.partial(pack_kernel, held_count=held_count), out...  2.12 us
    pallas_call x1, Pallas kernels, mix(): pl.pallas_call(mix_kernel, out_shape=jax.ShapeDtypeStruct((tokens, 2 * wi...  1.02 us
  transfers between devices with their start and end apart: 13, of which 2 were waited for; matrix products, arithmetic and copies ran while one was open for 0% of the time, Pallas kernels for 7%

profile of v3, /device:TPU:0, one launch (start us, length us, event | category | flops | bytes accessed | tf_op | source)
XLA Modules:
  0.0 31.6 jit_solution(4470801702379866613)
XLA Ops:
  0.0 2.1 %shard_map.64 = (bf16[8,128]{1,0:T(8,128)(2,1)S(1)}, bf16[24,1024]{1,0:T(8,128)(2,1)S(1)}, bf16[24,1024]{1,0:T(8,128)(2,1)S(1)}, bf16[2,2048,256]{2,1,0:T(8,128)(2,1)S(1)}, bf16[256,2048]{1,0:T(8,128)(2,1)S(1)}) custom-call(s32[1]{0:T(128)} %bitcast.base_ref, s32[8,128]{1,0:T(8,128)} %bitcast.14, f32[8,128]{1,0:T(8,128)} %bitcast.15, ...), custom_call_target="tpu_custom_call" | custom-call | tf_op jit(solution)/shard_map/pallas_call | solution.py:116
  2.1 3.0 %collective-permute-start = (bf16[24,1024]{1,0:T(8,128)(2,1)S(1)}, bf16[24,1024]{1,0:T(8,128)(2,1)S(1)}, u32[]{:S(2)}, u32[]{:S(2)}) collective-permute-start(bf16[24,1024]{1,0:T(8,128)(2,1)S(1)} %get-tuple-element.15), channel_id=1, source_target_pairs={{0,1},{1,0},{2,3},{3,2},{4,5},{5,4},{6,7},{7,6},{8,9},{9,8},{10,11... | collective-permute-start | bytes 147464 | tf_op jit(solution)/shard_map/ppermute | solution.py:258
  5.1 2.6 %collective-permute-start.3 = (bf16[24,1024]{1,0:T(8,128)(2,1)S(1)}, bf16[24,1024]{1,0:T(8,128)(2,1)S(1)}, u32[]{:S(2)}, u32[]{:S(2)}) collective-permute-start(bf16[24,1024]{1,0:T(8,128)(2,1)S(1)} %get-tuple-element.14.refs_0_), channel_id=1, source_target_pairs={{0,4},{2,6},{4,0},{6,2},{1,5},{3,7},{5,1},{7,3},{8,12},{10,14},{12... | collective-permute-start | bytes 147464 | tf_op jit(solution)/shard_map/ppermute | solution.py:258
  7.7 0.0 collective-permute-done.refs_1_
  7.7 2.6 %collective-permute-start.4 = (bf16[24,1024]{1,0:T(8,128)(2,1)S(1)}, bf16[24,1024]{1,0:T(8,128)(2,1)S(1)}, u32[]{:S(2)}, u32[]{:S(2)}) collective-permute-start(bf16[24,1024]{1,0:T(8,128)(2,1)S(1)} %collective-permute-done.refs_1_), channel_id=1, source_target_pairs={{0,4},{2,6},{4,0},{6,2},{1,5},{3,7},{5,1},{7,3},{8,12},{10,14},{12... | collective-permute-start | bytes 147464 | tf_op jit(solution)/shard_map/ppermute | solution.py:258
  10.3 1.3 %collective-permute-start.6 = (bf16[24,1024]{1,0:T(8,128)(2,1)S(1)}, bf16[24,1024]{1,0:T(8,128)(2,1)S(1)}, u32[]{:S(2)}, u32[]{:S(2)}) collective-permute-start(bf16[24,1024]{1,0:T(8,128)(2,1)S(1)} %get-tuple-element.14.refs_0_), channel_id=1, source_target_pairs={{0,6},{2,4},{4,2},{6,0},{1,7},{3,5},{5,3},{7,1},{8,14},{10,12},{12... | collective-permute-start | bytes 147464 | tf_op jit(solution)/shard_map/ppermute | solution.py:258
  11.7 2.5 %collective-permute-start.7 = (bf16[24,1024]{1,0:T(8,128)(2,1)S(1)}, bf16[24,1024]{1,0:T(8,128)(2,1)S(1)}, u32[]{:S(2)}, u32[]{:S(2)}) collective-permute-start(bf16[24,1024]{1,0:T(8,128)(2,1)S(1)} %collective-permute-done.refs_1_), channel_id=1, source_target_pairs={{0,6},{2,4},{4,2},{6,0},{1,7},{3,5},{5,3},{7,1},{8,14},{10,12},{12... | collective-permute-start | bytes 147464 | tf_op jit(solution)/shard_map/ppermute | solution.py:258
  14.1 0.0 collective-permute-start.1
  14.2 0.0 collective-permute-done.3.refs_0_
  14.2 2.0 %collective-permute-start.2 = (bf16[24,1024]{1,0:T(8,128)(2,1)S(1)}, bf16[24,1024]{1,0:T(8,128)(2,1)S(1)}, u32[]{:S(2)}, u32[]{:S(2)}) collective-permute-start(bf16[24,1024]{1,0:T(8,128)(2,1)S(1)} %collective-permute-done.refs_1_), channel_id=1, source_target_pairs={{0,2},{2,0},{4,6},{6,4},{1,3},{3,1},{5,7},{7,5},{8,10},{10,8},{12,... | collective-permute-start | bytes 147464 | tf_op jit(solution)/shard_map/ppermute | solution.py:258
  16.2 0.0 collective-permute-done.4.refs_1_
  16.2 0.7 %shard_map.66 = bf16[48,1024]{1,0:T(8,128)(2,1)S(1)} custom-call(bf16[2,2048,256]{2,1,0:T(8,128)(2,1)S(1)} %get-tuple-element.12.gate_up_ref, bf16[256,2048]{1,0:T(8,128)(2,1)S(1)} %get-tuple-element.13.down_ref, bf16[24,1024]{1,0:T(8,128)(2,1)S(1)} %collective-permute-done.3.refs_0_, bf16[24,1024]{1,0:T(8,128)(2,1)S(1)} %collective-permute-done.4.refs_1_), custom_call_target="tpu_custom_call" | custom-call | tf_op jit(solution)/shard_map/pallas_call | solution.py:155
  16.9 0.7 %collective-permute-start.5 = (bf16[48,1024]{1,0:T(8,128)(2,1)S(1)}, bf16[48,1024]{1,0:T(8,128)(2,1)S(1)}, u32[]{:S(2)}, u32[]{:S(2)}) collective-permute-start(bf16[48,1024]{1,0:T(8,128)(2,1)S(1)} %shard_map.66), channel_id=1, source_target_pairs={{0,4},{2,6},{4,0},{6,2},{1,5},{3,7},{5,1},{7,3},{8,12},{10,14},{12... | collective-permute-start | bytes 294920 | tf_op jit(solution)/shard_map/ppermute | solution.py:258
  17.6 0.0 collective-permute-done.6.refs_0_
  17.6 0.0 collective-permute-done.7.refs_1_
  17.6 0.7 %shard_map.67 = bf16[48,1024]{1,0:T(8,128)(2,1)S(1)} custom-call(bf16[2,2048,256]{2,1,0:T(8,128)(2,1)S(1)} %get-tuple-element.12.gate_up_ref, bf16[256,2048]{1,0:T(8,128)(2,1)S(1)} %get-tuple-element.13.down_ref, bf16[24,1024]{1,0:T(8,128)(2,1)S(1)} %collective-permute-done.6.refs_0_, bf16[24,1024]{1,0:T(8,128)(2,1)S(1)} %collective-permute-done.7.refs_1_), custom_call_target="tpu_custom_call" | custom-call | tf_op jit(solution)/shard_map/pallas_call | solution.py:155
  18.4 3.1 %collective-permute-start.8 = (bf16[48,1024]{1,0:T(8,128)(2,1)S(1)}, bf16[48,1024]{1,0:T(8,128)(2,1)S(1)}, u32[]{:S(2)}, u32[]{:S(2)}) collective-permute-start(bf16[48,1024]{1,0:T(8,128)(2,1)S(1)} %shard_map.67), channel_id=1, source_target_pairs={{0,6},{2,4},{4,2},{6,0},{1,7},{3,5},{5,3},{7,1},{8,14},{10,12},{12... | collective-permute-start | bytes 294920 | tf_op jit(solution)/shard_map/ppermute | solution.py:258
  21.5 0.0 collective-permute-done.1.refs_2_
  21.5 0.0 collective-permute-done.2.refs_3_
  21.5 0.7 %shard_map.65 = (bf16[48,1024]{1,0:T(8,128)(2,1)S(1)}, bf16[48,1024]{1,0:T(8,128)(2,1)S(1)}) custom-call(bf16[2,2048,256]{2,1,0:T(8,128)(2,1)S(1)} %get-tuple-element.12.gate_up_ref, bf16[256,2048]{1,0:T(8,128)(2,1)S(1)} %get-tuple-element.13.down_ref, bf16[24,1024]{1,0:T(8,128)(2,1)S(1)} %get-tuple-element.14.refs_0_, ...), custom_call_target="tpu_custom_call" | custom-call | tf_op jit(solution)/shard_map/pallas_call | solution.py:155
  22.2 0.1 collective-permute-start.12
  22.3 3.6 %collective-permute-start.10 = (bf16[24,1024]{1,0:T(8,128)(2,1)S(1)}, bf16[24,1024]{1,0:T(8,128)(2,1)S(1)}, u32[]{:S(2)}, u32[]{:S(2)}) collective-permute-start(bf16[24,1024]{1,0:T(8,128)(2,1)S(1)} %get-tuple-element.22), channel_id=1, source_target_pairs={{0,10},{2,8},{4,14},{6,12},{8,18},{10,16},{12,22},{14,20},{16,26},... | collective-permute-start | bytes 147464 | tf_op jit(solution)/shard_map/ppermute | solution.py:258
  25.9 0.0 collective-permute-done.5
  25.9 0.0 collective-permute-done.8
  25.9 0.1 collective-permute-start.11
  26.0 1.8 %collective-permute-start.9 = (bf16[32,1024]{1,0:T(8,128)(2,1)S(1)}, bf16[32,1024]{1,0:T(8,128)(2,1)S(1)}, u32[]{:S(2)}, u32[]{:S(2)}) collective-permute-start(bf16[32,1024]{1,0:T(8,128)(2,1)S(1)} %fusion.1), channel_id=1, source_target_pairs={{0,8},{8,16},{16,24},{24,0},{1,9},{9,17},{17,25},{25,1},{2,10},{10... | collective-permute-start | bytes 196616 | tf_op jit(solution)/shard_map/ppermute | solution.py:258
  27.8 0.2 collective-permute-done.12
  27.9 2.5 %collective-permute-done.11 = bf16[24,1024]{1,0:T(8,128)(2,1)S(1)} collective-permute-done((bf16[24,1024]{1,0:T(8,128)(2,1)S(1)}, bf16[24,1024]{1,0:T(8,128)(2,1)S(1)}, u32[]{:S(2)}, u32[]{:S(2)}) %collective-permute-start.11) | collective-permute-done | bytes 49184 | tf_op jit(solution)/shard_map/ppermute | solution.py:258
  30.4 0.0 collective-permute-done.9
  30.4 0.1 shard_map.68.table_ref
  30.6 0.0 collective-permute-done.10
  30.6 1.0 %shard_map.69 = bf16[128,2048]{1,0:T(8,128)(2,1)} custom-call(bf16[128,144]{1,0:T(8,128)(2,1)S(1)} %shard_map.68.table_ref, bf16[24,1024]{1,0:T(8,128)(2,1)S(1)} %add_convert_fusion.2.refs_0_, bf16[24,1024]{1,0:T(8,128)(2,1)S(1)} %add_convert_fusion.1.refs_1_), custom_call_target="tpu_custom_call" | custom-call | tf_op jit(solution)/shard_map/pallas_call | solution.py:233
  (7 shorter events, 0.1 us)
Async XLA Ops:
  2.1 5.6 %collective-permute-start = (bf16[24,1024]{1,0:T(8,128)(2,1)S(1)}, bf16[24,1024]{1,0:T(8,128)(2,1)S(1)}, u32[]{:S(2)}, u32[]{:S(2)}) collective-permute-start(bf16[24,1024]{1,0:T(8,128)(2,1)S(1)} %get-tuple-element.15), channel_id=1, source_target_pairs={{0,1},{1,0},{2,3},{3,2},{4,5},{5,4},{6,7},{7,6},{8,9},{9,8},{10,11... | collective-permute-start | bytes 147464 | tf_op jit(solution)/shard_map/ppermute | solution.py:258
  5.1 9.0 %collective-permute-start.3 = (bf16[24,1024]{1,0:T(8,128)(2,1)S(1)}, bf16[24,1024]{1,0:T(8,128)(2,1)S(1)}, u32[]{:S(2)}, u32[]{:S(2)}) collective-permute-start(bf16[24,1024]{1,0:T(8,128)(2,1)S(1)} %get-tuple-element.14.refs_0_), channel_id=1, source_target_pairs={{0,4},{2,6},{4,0},{6,2},{1,5},{3,7},{5,1},{7,3},{8,12},{10,14},{12... | collective-permute-start | bytes 147464 | tf_op jit(solution)/shard_map/ppermute | solution.py:258
  7.7 8.5 %collective-permute-start.4 = (bf16[24,1024]{1,0:T(8,128)(2,1)S(1)}, bf16[24,1024]{1,0:T(8,128)(2,1)S(1)}, u32[]{:S(2)}, u32[]{:S(2)}) collective-permute-start(bf16[24,1024]{1,0:T(8,128)(2,1)S(1)} %collective-permute-done.refs_1_), channel_id=1, source_target_pairs={{0,4},{2,6},{4,0},{6,2},{1,5},{3,7},{5,1},{7,3},{8,12},{10,14},{12... | collective-permute-start | bytes 147464 | tf_op jit(solution)/shard_map/ppermute | solution.py:258
  10.3 7.3 %collective-permute-start.6 = (bf16[24,1024]{1,0:T(8,128)(2,1)S(1)}, bf16[24,1024]{1,0:T(8,128)(2,1)S(1)}, u32[]{:S(2)}, u32[]{:S(2)}) collective-permute-start(bf16[24,1024]{1,0:T(8,128)(2,1)S(1)} %get-tuple-element.14.refs_0_), channel_id=1, source_target_pairs={{0,6},{2,4},{4,2},{6,0},{1,7},{3,5},{5,3},{7,1},{8,14},{10,12},{12... | collective-permute-start | bytes 147464 | tf_op jit(solution)/shard_map/ppermute | solution.py:258
  11.7 5.9 %collective-permute-start.7 = (bf16[24,1024]{1,0:T(8,128)(2,1)S(1)}, bf16[24,1024]{1,0:T(8,128)(2,1)S(1)}, u32[]{:S(2)}, u32[]{:S(2)}) collective-permute-start(bf16[24,1024]{1,0:T(8,128)(2,1)S(1)} %collective-permute-done.refs_1_), channel_id=1, source_target_pairs={{0,6},{2,4},{4,2},{6,0},{1,7},{3,5},{5,3},{7,1},{8,14},{10,12},{12... | collective-permute-start | bytes 147464 | tf_op jit(solution)/shard_map/ppermute | solution.py:258
  14.1 7.3 %collective-permute-start.1 = (bf16[24,1024]{1,0:T(8,128)(2,1)S(1)}, bf16[24,1024]{1,0:T(8,128)(2,1)S(1)}, u32[]{:S(2)}, u32[]{:S(2)}) collective-permute-start(bf16[24,1024]{1,0:T(8,128)(2,1)S(1)} %get-tuple-element.14.refs_0_), channel_id=1, source_target_pairs={{0,2},{2,0},{4,6},{6,4},{1,3},{3,1},{5,7},{7,5},{8,10},{10,8},{12,... | collective-permute-start | bytes 147464 | tf_op jit(solution)/shard_map/ppermute | solution.py:258
  14.2 7.3 %collective-permute-start.2 = (bf16[24,1024]{1,0:T(8,128)(2,1)S(1)}, bf16[24,1024]{1,0:T(8,128)(2,1)S(1)}, u32[]{:S(2)}, u32[]{:S(2)}) collective-permute-start(bf16[24,1024]{1,0:T(8,128)(2,1)S(1)} %collective-permute-done.refs_1_), channel_id=1, source_target_pairs={{0,2},{2,0},{4,6},{6,4},{1,3},{3,1},{5,7},{7,5},{8,10},{10,8},{12,... | collective-permute-start | bytes 147464 | tf_op jit(solution)/shard_map/ppermute | solution.py:258
  16.9 8.9 %collective-permute-start.5 = (bf16[48,1024]{1,0:T(8,128)(2,1)S(1)}, bf16[48,1024]{1,0:T(8,128)(2,1)S(1)}, u32[]{:S(2)}, u32[]{:S(2)}) collective-permute-start(bf16[48,1024]{1,0:T(8,128)(2,1)S(1)} %shard_map.66), channel_id=1, source_target_pairs={{0,4},{2,6},{4,0},{6,2},{1,5},{3,7},{5,1},{7,3},{8,12},{10,14},{12... | collective-permute-start | bytes 294920 | tf_op jit(solution)/shard_map/ppermute | solution.py:258
  18.4 7.5 %collective-permute-start.8 = (bf16[48,1024]{1,0:T(8,128)(2,1)S(1)}, bf16[48,1024]{1,0:T(8,128)(2,1)S(1)}, u32[]{:S(2)}, u32[]{:S(2)}) collective-permute-start(bf16[48,1024]{1,0:T(8,128)(2,1)S(1)} %shard_map.67), channel_id=1, source_target_pairs={{0,6},{2,4},{4,2},{6,0},{1,7},{3,5},{5,3},{7,1},{8,14},{10,12},{12... | collective-permute-start | bytes 294920 | tf_op jit(solution)/shard_map/ppermute | solution.py:258
  22.2 5.7 %collective-permute-start.12 = (bf16[24,1024]{1,0:T(8,128)(2,1)S(1)}, bf16[24,1024]{1,0:T(8,128)(2,1)S(1)}, u32[]{:S(2)}, u32[]{:S(2)}) collective-permute-start(bf16[24,1024]{1,0:T(8,128)(2,1)S(1)} %get-tuple-element.21), channel_id=1, source_target_pairs={{0,11},{1,10},{2,9},{3,8},{4,15},{5,14},{6,13},{7,12},{8,19},{9,18... | collective-permute-start | bytes 147464 | tf_op jit(solution)/shard_map/ppermute | solution.py:258
  22.3 8.2 %collective-permute-start.10 = (bf16[24,1024]{1,0:T(8,128)(2,1)S(1)}, bf16[24,1024]{1,0:T(8,128)(2,1)S(1)}, u32[]{:S(2)}, u32[]{:S(2)}) collective-permute-start(bf16[24,1024]{1,0:T(8,128)(2,1)S(1)} %get-tuple-element.22), channel_id=1, source_target_pairs={{0,10},{2,8},{4,14},{6,12},{8,18},{10,16},{12,22},{14,20},{16,26},... | collective-permute-start | bytes 147464 | tf_op jit(solution)/shard_map/ppermute | solution.py:258
  25.9 4.5 %collective-permute-start.11 = (bf16[24,1024]{1,0:T(8,128)(2,1)S(1)}, bf16[24,1024]{1,0:T(8,128)(2,1)S(1)}, u32[]{:S(2)}, u32[]{:S(2)}) collective-permute-start(bf16[24,1024]{1,0:T(8,128)(2,1)S(1)} %get-tuple-element.19), channel_id=1, source_target_pairs={{0,9},{1,8},{8,17},{9,16},{16,25},{17,24},{24,1},{25,0},{2,11},{3,... | collective-permute-start | bytes 147464 | tf_op jit(solution)/shard_map/ppermute | solution.py:258
  26.0 4.4 %collective-permute-start.9 = (bf16[32,1024]{1,0:T(8,128)(2,1)S(1)}, bf16[32,1024]{1,0:T(8,128)(2,1)S(1)}, u32[]{:S(2)}, u32[]{:S(2)}) collective-permute-start(bf16[32,1024]{1,0:T(8,128)(2,1)S(1)} %fusion.1), channel_id=1, source_target_pairs={{0,8},{8,16},{16,24},{24,0},{1,9},{9,17},{17,25},{25,1},{2,10},{10... | collective-permute-start | bytes 196616 | tf_op jit(solution)/shard_map/ppermute | solution.py:258

commit v4 on v3

--- a/solution.py
+++ b/solution.py
@@ -15,6 +15,7 @@
 LOAD_PIECES = 2
 MIX_PIECES = 2
 VMEM_LIMIT = 40 * 1024 * 1024
+LIGHT = pl.CostEstimate(flops=1, bytes_accessed=1, transcendentals=0)
 
 
 def row_tables(rows, lanes):
@@ -157,6 +158,7 @@
         out_shape=[jax.ShapeDtypeStruct((count, width), bf16) for count in out_rows],
         in_specs=[whole] * (2 + len(blocks)),
         out_specs=[whole] * len(out_rows),
+        cost_estimate=LIGHT,
         compiler_params=pltpu.CompilerParams(vmem_limit_bytes=VMEM_LIMIT),
     )(gate_up, down, *blocks)
 
@@ -182,43 +184,29 @@
     )(gate_up, down, block)
 
 
-def table_kernel(meta_ref, table_ref, *, held_count):
-    tokens = table_ref.shape[0]
+def mix_kernel(meta_ref, *refs, held_count):
+    rows_refs, out_hbm, out_ref, sems = refs[:-3], refs[-3], refs[-2], refs[-1]
+    tokens, width = out_ref.shape
+    half = width // 2
     meta = meta_ref[:, :tokens].astype(f32)
     _, slot = row_tables(GROUP, tokens)
+    values = jnp.concatenate([ref[...].astype(f32) for ref in rows_refs], axis=0)
+    left, _ = row_tables(*values.shape)
+    sides = [jnp.where(left, values, 0.0).astype(bf16), jnp.where(left, 0.0, values).astype(bf16)]
     lines = []
     for piece in range(3):
         for block in range(held_count):
             position = meta[4 * block + 3 : 4 * block + 4]
             share = meta[4 * block + piece : 4 * block + piece + 1]
             lines.append(jnp.where(slot.astype(f32) == position, share, 0.0))
-    table_ref[...] = jnp.concatenate(lines, axis=0).T.astype(bf16)
-
-
-def share_table(meta, tokens, held_count):
-    whole = pl.BlockSpec(memory_space=pltpu.VMEM)
-    return pl.pallas_call(
-        functools.partial(table_kernel, held_count=held_count),
-        out_shape=jax.ShapeDtypeStruct((tokens, 3 * GROUP * held_count), bf16),
-        in_specs=[whole],
-        out_specs=whole,
-        compiler_params=pltpu.CompilerParams(vmem_limit_bytes=VMEM_LIMIT),
-    )(meta)
-
-
-def mix_kernel(table_ref, *refs):
-    rows_refs, out_hbm, out_ref, sems = refs[:-3], refs[-3], refs[-2], refs[-1]
-    half = out_ref.shape[1] // 2
-    values = jnp.concatenate([ref[...].astype(f32) for ref in rows_refs], axis=0)
-    left, _ = row_tables(*values.shape)
-    sides = [jnp.where(left, values, 0.0).astype(bf16), jnp.where(left, 0.0, values).astype(bf16)]
+    table = jnp.concatenate(lines, axis=0).T.astype(bf16)
     copies = []
     for step in range(2 * MIX_PIECES):
         side, piece = divmod(step, MIX_PIECES)
         length = half // MIX_PIECES
         columns = pl.ds(step * length, length)
         value = sides[side][:, piece * length : (piece + 1) * length]
-        total = dot(table_ref[...], jnp.concatenate([value] * 3, axis=0))
+        total = dot(table, jnp.concatenate([value] * 3, axis=0))
         out_ref[:, columns] = total.astype(bf16)
         copies.append(pltpu.make_async_copy(out_ref.at[:, columns], out_hbm.at[:, columns], sems.at[step]))
         copies[step].start()
@@ -226,18 +214,17 @@
         copy.wait()
 
 
-def mix(table, blocks):
-    tokens = table.shape[0]
+def mix(meta, blocks, tokens, held_count):
     width = blocks[0].shape[1]
     whole = pl.BlockSpec(memory_space=pltpu.VMEM)
     return pl.pallas_call(
-        mix_kernel,
+        functools.partial(mix_kernel, held_count=held_count),
         out_shape=jax.ShapeDtypeStruct((tokens, 2 * width), bf16),
         in_specs=[whole] * (1 + len(blocks)),
         out_specs=pl.BlockSpec(memory_space=pltpu.HBM),
         scratch_shapes=[pltpu.VMEM((tokens, 2 * width), bf16), pltpu.SemaphoreType.DMA((2 * MIX_PIECES,))],
         compiler_params=pltpu.CompilerParams(vmem_limit_bytes=VMEM_LIMIT),
-    )(table, *blocks)
+    )(meta, *blocks)
 
 
 def move(value, axes, target):
@@ -276,19 +263,17 @@
     blocks = {0: [own, other]}
     for step in (3, 2, 1):
         blocks[step] = [across(own, step), across(other, step)]
-    rows = 2 * GROUP
-    part0, part1 = expert_quarter(blocks[0] + blocks[1], [rows, rows], gate_up, down)
-    back2 = across(expert_quarter(blocks[2], [rows], gate_up, down)[0], 2)
-    back3 = across(expert_quarter(blocks[3], [rows], gate_up, down)[0], 3)
-    direct = move(part1[:GROUP], ("section", "dp"), lambda s, q: (s + 1, q ^ 1))
-    direct_crossed = move(part1[GROUP:], ("section", "dp", "expert"), lambda s, q, e: (s + 1, q ^ 1, e ^ 1))
-    summed = added([part0, back2, back3])
+    rows = [2 * GROUP] * 2
+    part1, part3 = expert_quarter(blocks[1] + blocks[3], rows, gate_up, down)
+    part0, part2 = expert_quarter(blocks[0] + blocks[2], rows, gate_up, down)
+    summed = added([part0, across(part1, 1), across(part3, 3)])
+    direct = move(part2[:GROUP], ("section", "dp"), lambda s, q: (s + 1, q ^ 2))
+    direct_crossed = move(part2[GROUP:], ("section", "dp", "expert"), lambda s, q, e: (s + 1, q ^ 2, e ^ 1))
     wide = jnp.pad(meta, ((0, 0), (0, summed.shape[1] - meta.shape[1])))
     tagged = jnp.concatenate([summed[:GROUP], wide], axis=0)
     tagged = move(tagged, ("section",), lambda s: (s + 1,))
     crossed = move(summed[GROUP:], ("section", "expert"), lambda s, e: (s + 1, e ^ 1))
-    table = share_table(tagged[GROUP:], stream.shape[0], 2)
-    return mix(table, [added([tagged[:GROUP], direct]), added([crossed, direct_crossed])])
+    return mix(tagged[GROUP:], [added([tagged[:GROUP], direct]), added([crossed, direct_crossed])], stream.shape[0], 2)
 
 
 def many_shards(stream, gain, probs, ids, gate_up, down):
@@ -311,7 +296,7 @@
     for step in range(1, group_count):
         parts.append(shifted(expert_quarter_many(shifted(received, step), gate_up, down), -step))
     summed = move(exchanged(added(parts)), ("section",), lambda s: (s + 1,))
-    return mix(share_table(meta, stream.shape[0], held_count), [summed])
+    return mix(meta, [summed], stream.shape[0], held_count)
 
 
 def shards(stream, norm_gain, gate_probs, expert_ids, gate_up_weight, down_weight):

time: 31.8 us -> 31 us (0.975)
  starting transfers between devices: 23.3 us -> 21.4 us
  waiting for transfers between devices: 2.66 us -> 4.51 us
  Pallas kernels: 5.47 us -> 4.68 us
    ppermute x13, waiting for transfers between devices: 2.66 us -> 4.51 us  [move(): return lax.ppermute(value, axes if len(axes) > 1 else axes[0], pairs)]
    ppermute x13, starting transfers between devices: 23.3 us -> 21.4 us  [move(): return lax.ppermute(value, axes if len(axes) > 1 else axes[0], pairs)]
    pallas_call x3 -> x2, Pallas kernels: 2.22 us -> 1.48 us  [expert_quarter(): pl.pallas_call(functools.partial(expert_kernel, count=len(blocks)), out_s...]
    pallas_call x2 -> x1, Pallas kernels: 1.13 us -> 1.07 us  [mix(): pl.pallas_call(functools.partial(mix_kernel, held_count=held_count), out_...]
  transfers between devices with their start and end apart: 13 -> 13, of which waited for: 2 -> 6; matrix products, arithmetic and copies ran while one was open for 0% -> 0% of each run, Pallas kernels for 7% -> 5%
where the time goes in v4:
time: 31 us; the launch traced here: 30.8 us
  starting transfers between devices  21.4 us (69%)
  Pallas kernels  4.68 us (15%)
  waiting for transfers between devices  4.51 us (15%)
    ppermute x13, starting transfers between devices, move(): return lax.ppermute(value, axes if len(axes) > 1 else axes[0], pairs)  21.4 us
    ppermute x13, waiting for transfers between devices, move(): return lax.ppermute(value, axes if len(axes) > 1 else axes[0], pairs)  4.51 us
    pallas_call x1, Pallas kernels, pack(): pl.pallas_call(functools.partial(pack_kernel, held_count=held_count), out...  2.12 us
    pallas_call x2, Pallas kernels, expert_quarter(): pl.pallas_call(functools.partial(expert_kernel, count=len(blocks)), out_s...  1.48 us
    pallas_call x1, Pallas kernels, mix(): pl.pallas_call(functools.partial(mix_kernel, held_count=held_count), out_...  1.07 us
  transfers between devices with their start and end apart: 13, of which 6 were waited for; matrix products, arithmetic and copies ran while one was open for 0% of the time, Pallas kernels for 5%

profile of v4, /device:TPU:0, one launch (start us, length us, event | category | flops | bytes accessed | tf_op | source)
XLA Modules:
  0.0 30.8 jit_solution(10260871660804583192)
XLA Ops:
  0.0 2.1 %shard_map.64 = (bf16[8,128]{1,0:T(8,128)(2,1)S(1)}, bf16[24,1024]{1,0:T(8,128)(2,1)S(1)}, bf16[24,1024]{1,0:T(8,128)(2,1)S(1)}, bf16[2,2048,256]{2,1,0:T(8,128)(2,1)S(1)}, bf16[256,2048]{1,0:T(8,128)(2,1)S(1)}) custom-call(s32[1]{0:T(128)} %bitcast.base_ref, s32[8,128]{1,0:T(8,128)} %bitcast.14, f32[8,128]{1,0:T(8,128)} %bitcast.15, ...), custom_call_target="tpu_custom_call" | custom-call | tf_op jit(solution)/shard_map/pallas_call | solution.py:117
  2.1 3.0 %collective-permute-start = (bf16[24,1024]{1,0:T(8,128)(2,1)S(1)}, bf16[24,1024]{1,0:T(8,128)(2,1)S(1)}, u32[]{:S(2)}, u32[]{:S(2)}) collective-permute-start(bf16[24,1024]{1,0:T(8,128)(2,1)S(1)} %get-tuple-element.17), channel_id=1, source_target_pairs={{0,1},{1,0},{2,3},{3,2},{4,5},{5,4},{6,7},{7,6},{8,9},{9,8},{10,11... | collective-permute-start | bytes 147464 | tf_op jit(solution)/shard_map/ppermute | solution.py:245
  5.1 3.6 %collective-permute-start.5 = (bf16[24,1024]{1,0:T(8,128)(2,1)S(1)}, bf16[24,1024]{1,0:T(8,128)(2,1)S(1)}, u32[]{:S(2)}, u32[]{:S(2)}) collective-permute-start(bf16[24,1024]{1,0:T(8,128)(2,1)S(1)} %get-tuple-element.16.refs_0_), channel_id=1, source_target_pairs={{0,6},{2,4},{4,2},{6,0},{1,7},{3,5},{5,3},{7,1},{8,14},{10,12},{12... | collective-permute-start | bytes 147464 | tf_op jit(solution)/shard_map/ppermute | solution.py:245
  8.7 0.0 collective-permute-start.3
  8.7 0.0 collective-permute-done.refs_1_
  8.7 2.6 %collective-permute-start.6 = (bf16[24,1024]{1,0:T(8,128)(2,1)S(1)}, bf16[24,1024]{1,0:T(8,128)(2,1)S(1)}, u32[]{:S(2)}, u32[]{:S(2)}) collective-permute-start(bf16[24,1024]{1,0:T(8,128)(2,1)S(1)} %collective-permute-done.refs_1_), channel_id=1, source_target_pairs={{0,6},{2,4},{4,2},{6,0},{1,7},{3,5},{5,3},{7,1},{8,14},{10,12},{12... | collective-permute-start | bytes 147464 | tf_op jit(solution)/shard_map/ppermute | solution.py:245
  11.3 0.0 collective-permute-start.4
  11.3 1.8 %collective-permute-start.1 = (bf16[24,1024]{1,0:T(8,128)(2,1)S(1)}, bf16[24,1024]{1,0:T(8,128)(2,1)S(1)}, u32[]{:S(2)}, u32[]{:S(2)}) collective-permute-start(bf16[24,1024]{1,0:T(8,128)(2,1)S(1)} %get-tuple-element.16.refs_0_), channel_id=1, source_target_pairs={{0,4},{2,6},{4,0},{6,2},{1,5},{3,7},{5,1},{7,3},{8,12},{10,14},{12... | collective-permute-start | bytes 147464 | tf_op jit(solution)/shard_map/ppermute | solution.py:245
  13.1 0.0 collective-permute-done.5.refs_2_
  13.1 1.1 %collective-permute-start.2 = (bf16[24,1024]{1,0:T(8,128)(2,1)S(1)}, bf16[24,1024]{1,0:T(8,128)(2,1)S(1)}, u32[]{:S(2)}, u32[]{:S(2)}) collective-permute-start(bf16[24,1024]{1,0:T(8,128)(2,1)S(1)} %collective-permute-done.refs_1_), channel_id=1, source_target_pairs={{0,4},{2,6},{4,0},{6,2},{1,5},{3,7},{5,1},{7,3},{8,12},{10,14},{12... | collective-permute-start | bytes 147464 | tf_op jit(solution)/shard_map/ppermute | solution.py:245
  14.3 0.6 %collective-permute-done.3.refs_0_ = bf16[24,1024]{1,0:T(8,128)(2,1)S(1)} collective-permute-done((bf16[24,1024]{1,0:T(8,128)(2,1)S(1)}, bf16[24,1024]{1,0:T(8,128)(2,1)S(1)}, u32[]{:S(2)}, u32[]{:S(2)}) %collective-permute-start.3) | collective-permute-done | bytes 49184 | tf_op jit(solution)/shard_map/ppermute | solution.py:245
  14.8 0.1 collective-permute-done.6.refs_3_
  15.0 0.6 %collective-permute-done.4.refs_1_ = bf16[24,1024]{1,0:T(8,128)(2,1)S(1)} collective-permute-done((bf16[24,1024]{1,0:T(8,128)(2,1)S(1)}, bf16[24,1024]{1,0:T(8,128)(2,1)S(1)}, u32[]{:S(2)}, u32[]{:S(2)}) %collective-permute-start.4) | collective-permute-done | bytes 49184 | tf_op jit(solution)/shard_map/ppermute | solution.py:245
  15.6 0.7 %shard_map.66 = (bf16[48,1024]{1,0:T(8,128)(2,1)S(1)}, bf16[48,1024]{1,0:T(8,128)(2,1)S(1)}) custom-call(bf16[2,2048,256]{2,1,0:T(8,128)(2,1)S(1)} %get-tuple-element.14.gate_up_ref, bf16[256,2048]{1,0:T(8,128)(2,1)S(1)} %get-tuple-element.15.down_ref, bf16[24,1024]{1,0:T(8,128)(2,1)S(1)} %collective-permute-done.3.refs_0_, ...), custom_call_target="tpu_custom_call" | custom-call | flops 1 | bytes 1 | tf_op jit(solution)/shard_map/pallas_call | solution.py:156
  16.3 1.1 %collective-permute-start.7 = (bf16[48,1024]{1,0:T(8,128)(2,1)S(1)}, bf16[48,1024]{1,0:T(8,128)(2,1)S(1)}, u32[]{:S(2)}, u32[]{:S(2)}) collective-permute-start(bf16[48,1024]{1,0:T(8,128)(2,1)S(1)} %get-tuple-element.19), channel_id=1, source_target_pairs={{0,2},{2,0},{4,6},{6,4},{1,3},{3,1},{5,7},{7,5},{8,10},{10,8},{12,... | collective-permute-start | bytes 294920 | tf_op jit(solution)/shard_map/ppermute | solution.py:245
  17.4 1.6 %collective-permute-start.8 = (bf16[48,1024]{1,0:T(8,128)(2,1)S(1)}, bf16[48,1024]{1,0:T(8,128)(2,1)S(1)}, u32[]{:S(2)}, u32[]{:S(2)}) collective-permute-start(bf16[48,1024]{1,0:T(8,128)(2,1)S(1)} %get-tuple-element.20), channel_id=1, source_target_pairs={{0,6},{2,4},{4,2},{6,0},{1,7},{3,5},{5,3},{7,1},{8,14},{10,12},{12... | collective-permute-start | bytes 294920 | tf_op jit(solution)/shard_map/ppermute | solution.py:245
  19.0 0.0 collective-permute-done.1.refs_2_
  19.0 0.0 collective-permute-done.2.refs_3_
  19.0 0.7 %shard_map.65 = (bf16[48,1024]{1,0:T(8,128)(2,1)S(1)}, bf16[48,1024]{1,0:T(8,128)(2,1)S(1)}) custom-call(bf16[2,2048,256]{2,1,0:T(8,128)(2,1)S(1)} %get-tuple-element.14.gate_up_ref, bf16[256,2048]{1,0:T(8,128)(2,1)S(1)} %get-tuple-element.15.down_ref, bf16[24,1024]{1,0:T(8,128)(2,1)S(1)} %get-tuple-element.16.refs_0_, ...), custom_call_target="tpu_custom_call" | custom-call | flops 1 | bytes 1 | tf_op jit(solution)/shard_map/pallas_call | solution.py:156
  19.8 0.1 collective-permute-start.12
  19.8 4.1 %collective-permute-start.10 = (bf16[24,1024]{1,0:T(8,128)(2,1)S(1)}, bf16[24,1024]{1,0:T(8,128)(2,1)S(1)}, u32[]{:S(2)}, u32[]{:S(2)}) collective-permute-start(bf16[24,1024]{1,0:T(8,128)(2,1)S(1)} %get-tuple-element.26), channel_id=1, source_target_pairs={{0,12},{2,14},{4,8},{6,10},{8,20},{10,22},{12,16},{14,18},{16,28},... | collective-permute-start | bytes 147464 | tf_op jit(solution)/shard_map/ppermute | solution.py:245
  24.0 0.0 collective-permute-done.7
  24.0 0.0 collective-permute-done.8
  24.0 0.1 collective-permute-start.11
  24.1 2.4 %collective-permute-start.9 = (bf16[32,1024]{1,0:T(8,128)(2,1)S(1)}, bf16[32,1024]{1,0:T(8,128)(2,1)S(1)}, u32[]{:S(2)}, u32[]{:S(2)}) collective-permute-start(bf16[32,1024]{1,0:T(8,128)(2,1)S(1)} %fusion.1), channel_id=1, source_target_pairs={{0,8},{8,16},{16,24},{24,0},{1,9},{9,17},{17,25},{25,1},{2,10},{10... | collective-permute-start | bytes 196616 | tf_op jit(solution)/shard_map/ppermute | solution.py:245
  26.5 2.5 %collective-permute-done.12 = bf16[24,1024]{1,0:T(8,128)(2,1)S(1)} collective-permute-done((bf16[24,1024]{1,0:T(8,128)(2,1)S(1)}, bf16[24,1024]{1,0:T(8,128)(2,1)S(1)}, u32[]{:S(2)}, u32[]{:S(2)}) %collective-permute-start.12) | collective-permute-done | bytes 49184 | tf_op jit(solution)/shard_map/ppermute | solution.py:245
  29.0 0.2 collective-permute-done.11
  29.2 0.5 %collective-permute-done.9 = bf16[32,1024]{1,0:T(8,128)(2,1)S(1)} collective-permute-done((bf16[32,1024]{1,0:T(8,128)(2,1)S(1)}, bf16[32,1024]{1,0:T(8,128)(2,1)S(1)}, u32[]{:S(2)}, u32[]{:S(2)}) %collective-permute-start.9) | collective-permute-done | bytes 65568 | tf_op jit(solution)/shard_map/ppermute | solution.py:245
  29.7 0.0 collective-permute-done.10
  29.7 1.1 %shard_map.67 = bf16[128,2048]{1,0:T(8,128)(2,1)} custom-call(bf16[8,1024]{1,0:T(8,128)(2,1)S(1)} %slice.25.meta_ref, bf16[24,1024]{1,0:T(8,128)(2,1)S(1)} %add_convert_fusion.2.refs_0_, bf16[24,1024]{1,0:T(8,128)(2,1)S(1)} %add_convert_fusion.1.refs_1_), custom_call_target="tpu_custom_call" | custom-call | tf_op jit(solution)/shard_map/pallas_call | solution.py:220
  (7 shorter events, 0.1 us)
Async XLA Ops:
  2.1 6.6 %collective-permute-start = (bf16[24,1024]{1,0:T(8,128)(2,1)S(1)}, bf16[24,1024]{1,0:T(8,128)(2,1)S(1)}, u32[]{:S(2)}, u32[]{:S(2)}) collective-permute-start(bf16[24,1024]{1,0:T(8,128)(2,1)S(1)} %get-tuple-element.17), channel_id=1, source_target_pairs={{0,1},{1,0},{2,3},{3,2},{4,5},{5,4},{6,7},{7,6},{8,9},{9,8},{10,11... | collective-permute-start | bytes 147464 | tf_op jit(solution)/shard_map/ppermute | solution.py:245
  5.1 8.0 %collective-permute-start.5 = (bf16[24,1024]{1,0:T(8,128)(2,1)S(1)}, bf16[24,1024]{1,0:T(8,128)(2,1)S(1)}, u32[]{:S(2)}, u32[]{:S(2)}) collective-permute-start(bf16[24,1024]{1,0:T(8,128)(2,1)S(1)} %get-tuple-element.16.refs_0_), channel_id=1, source_target_pairs={{0,6},{2,4},{4,2},{6,0},{1,7},{3,5},{5,3},{7,1},{8,14},{10,12},{12... | collective-permute-start | bytes 147464 | tf_op jit(solution)/shard_map/ppermute | solution.py:245
  8.7 6.1 %collective-permute-start.3 = (bf16[24,1024]{1,0:T(8,128)(2,1)S(1)}, bf16[24,1024]{1,0:T(8,128)(2,1)S(1)}, u32[]{:S(2)}, u32[]{:S(2)}) collective-permute-start(bf16[24,1024]{1,0:T(8,128)(2,1)S(1)} %get-tuple-element.16.refs_0_), channel_id=1, source_target_pairs={{0,2},{2,0},{4,6},{6,4},{1,3},{3,1},{5,7},{7,5},{8,10},{10,8},{12,... | collective-permute-start | bytes 147464 | tf_op jit(solution)/shard_map/ppermute | solution.py:245
  8.7 6.2 %collective-permute-start.6 = (bf16[24,1024]{1,0:T(8,128)(2,1)S(1)}, bf16[24,1024]{1,0:T(8,128)(2,1)S(1)}, u32[]{:S(2)}, u32[]{:S(2)}) collective-permute-start(bf16[24,1024]{1,0:T(8,128)(2,1)S(1)} %collective-permute-done.refs_1_), channel_id=1, source_target_pairs={{0,6},{2,4},{4,2},{6,0},{1,7},{3,5},{5,3},{7,1},{8,14},{10,12},{12... | collective-permute-start | bytes 147464 | tf_op jit(solution)/shard_map/ppermute | solution.py:245
  11.3 4.2 %collective-permute-start.4 = (bf16[24,1024]{1,0:T(8,128)(2,1)S(1)}, bf16[24,1024]{1,0:T(8,128)(2,1)S(1)}, u32[]{:S(2)}, u32[]{:S(2)}) collective-permute-start(bf16[24,1024]{1,0:T(8,128)(2,1)S(1)} %collective-permute-done.refs_1_), channel_id=1, source_target_pairs={{0,2},{2,0},{4,6},{6,4},{1,3},{3,1},{5,7},{7,5},{8,10},{10,8},{12,... | collective-permute-start | bytes 147464 | tf_op jit(solution)/shard_map/ppermute | solution.py:245
  11.3 7.7 %collective-permute-start.1 = (bf16[24,1024]{1,0:T(8,128)(2,1)S(1)}, bf16[24,1024]{1,0:T(8,128)(2,1)S(1)}, u32[]{:S(2)}, u32[]{:S(2)}) collective-permute-start(bf16[24,1024]{1,0:T(8,128)(2,1)S(1)} %get-tuple-element.16.refs_0_), channel_id=1, source_target_pairs={{0,4},{2,6},{4,0},{6,2},{1,5},{3,7},{5,1},{7,3},{8,12},{10,14},{12... | collective-permute-start | bytes 147464 | tf_op jit(solution)/shard_map/ppermute | solution.py:245
  13.1 5.9 %collective-permute-start.2 = (bf16[24,1024]{1,0:T(8,128)(2,1)S(1)}, bf16[24,1024]{1,0:T(8,128)(2,1)S(1)}, u32[]{:S(2)}, u32[]{:S(2)}) collective-permute-start(bf16[24,1024]{1,0:T(8,128)(2,1)S(1)} %collective-permute-done.refs_1_), channel_id=1, source_target_pairs={{0,4},{2,6},{4,0},{6,2},{1,5},{3,7},{5,1},{7,3},{8,12},{10,14},{12... | collective-permute-start | bytes 147464 | tf_op jit(solution)/shard_map/ppermute | solution.py:245
  16.3 7.7 %collective-permute-start.7 = (bf16[48,1024]{1,0:T(8,128)(2,1)S(1)}, bf16[48,1024]{1,0:T(8,128)(2,1)S(1)}, u32[]{:S(2)}, u32[]{:S(2)}) collective-permute-start(bf16[48,1024]{1,0:T(8,128)(2,1)S(1)} %get-tuple-element.19), channel_id=1, source_target_pairs={{0,2},{2,0},{4,6},{6,4},{1,3},{3,1},{5,7},{7,5},{8,10},{10,8},{12,... | collective-permute-start | bytes 294920 | tf_op jit(solution)/shard_map/ppermute | solution.py:245
  17.4 6.6 %collective-permute-start.8 = (bf16[48,1024]{1,0:T(8,128)(2,1)S(1)}, bf16[48,1024]{1,0:T(8,128)(2,1)S(1)}, u32[]{:S(2)}, u32[]{:S(2)}) collective-permute-start(bf16[48,1024]{1,0:T(8,128)(2,1)S(1)} %get-tuple-element.20), channel_id=1, source_target_pairs={{0,6},{2,4},{4,2},{6,0},{1,7},{3,5},{5,3},{7,1},{8,14},{10,12},{12... | collective-permute-start | bytes 294920 | tf_op jit(solution)/shard_map/ppermute | solution.py:245
  19.8 9.2 %collective-permute-start.12 = (bf16[24,1024]{1,0:T(8,128)(2,1)S(1)}, bf16[24,1024]{1,0:T(8,128)(2,1)S(1)}, u32[]{:S(2)}, u32[]{:S(2)}) collective-permute-start(bf16[24,1024]{1,0:T(8,128)(2,1)S(1)} %get-tuple-element.25), channel_id=1, source_target_pairs={{0,13},{1,12},{2,15},{3,14},{4,9},{5,8},{6,11},{7,10},{8,21},{9,20... | collective-permute-start | bytes 147464 | tf_op jit(solution)/shard_map/ppermute | solution.py:245
  19.8 9.9 %collective-permute-start.10 = (bf16[24,1024]{1,0:T(8,128)(2,1)S(1)}, bf16[24,1024]{1,0:T(8,128)(2,1)S(1)}, u32[]{:S(2)}, u32[]{:S(2)}) collective-permute-start(bf16[24,1024]{1,0:T(8,128)(2,1)S(1)} %get-tuple-element.26), channel_id=1, source_target_pairs={{0,12},{2,14},{4,8},{6,10},{8,20},{10,22},{12,16},{14,18},{16,28},... | collective-permute-start | bytes 147464 | tf_op jit(solution)/shard_map/ppermute | solution.py:245
  24.0 5.2 %collective-permute-start.11 = (bf16[24,1024]{1,0:T(8,128)(2,1)S(1)}, bf16[24,1024]{1,0:T(8,128)(2,1)S(1)}, u32[]{:S(2)}, u32[]{:S(2)}) collective-permute-start(bf16[24,1024]{1,0:T(8,128)(2,1)S(1)} %get-tuple-element.23), channel_id=1, source_target_pairs={{0,9},{1,8},{8,17},{9,16},{16,25},{17,24},{24,1},{25,0},{2,11},{3,... | collective-permute-start | bytes 147464 | tf_op jit(solution)/shard_map/ppermute | solution.py:245
  24.1 5.6 %collective-permute-start.9 = (bf16[32,1024]{1,0:T(8,128)(2,1)S(1)}, bf16[32,1024]{1,0:T(8,128)(2,1)S(1)}, u32[]{:S(2)}, u32[]{:S(2)}) collective-permute-start(bf16[32,1024]{1,0:T(8,128)(2,1)S(1)} %fusion.1), channel_id=1, source_target_pairs={{0,8},{8,16},{16,24},{24,0},{1,9},{9,17},{17,25},{25,1},{2,10},{10... | collective-permute-start | bytes 196616 | tf_op jit(solution)/shard_map/ppermute | solution.py:245

commit v5 on v4

--- a/solution.py
+++ b/solution.py
@@ -249,6 +249,10 @@
     return move(value, ("dp",), lambda q: (q ^ step,))
 
 
+def swapped_across(value, step):
+    return move(value, ("dp", "expert"), lambda q, e: (q ^ step, e ^ 1))
+
+
 def added(values):
     total = values[0].astype(f32)
     for value in values[1:]:
@@ -259,13 +263,14 @@
 def pair_shards(stream, gain, probs, ids, gate_up, down):
     base = lax.axis_index("expert").astype(jnp.int32).reshape(1)
     meta, own, other, gate_up, down = pack(stream, gain, probs, ids, gate_up, down, base, 2, 2)
+    mine = other
     other = move(other, ("expert",), lambda e: (e ^ 1,))
     blocks = {0: [own, other]}
     for step in (3, 2, 1):
-        blocks[step] = [across(own, step), across(other, step)]
+        blocks[step] = [across(own, step), swapped_across(mine, step)]
     rows = [2 * GROUP] * 2
+    part0, part2 = expert_quarter(blocks[0] + blocks[2], rows, gate_up, down)
     part1, part3 = expert_quarter(blocks[1] + blocks[3], rows, gate_up, down)
-    part0, part2 = expert_quarter(blocks[0] + blocks[2], rows, gate_up, down)
     summed = added([part0, across(part1, 1), across(part3, 3)])
     direct = move(part2[:GROUP], ("section", "dp"), lambda s, q: (s + 1, q ^ 2))
     direct_crossed = move(part2[GROUP:], ("section", "dp", "expert"), lambda s, q, e: (s + 1, q ^ 2, e ^ 1))

time: 31 us -> 31 us (level)
  transfers between devices with their start and end apart: 13 -> 13, of which waited for: 6 -> 3; matrix products, arithmetic and copies ran while one was open for 0% -> 0% of each run, Pallas kernels for 5% -> 5%
where the time goes in v5:
time: 31 us; the launch traced here: 30.8 us
  starting transfers between devices  21.7 us (70%)
  Pallas kernels  4.67 us (15%)
  waiting for transfers between devices  4.24 us (14%)
    ppermute x13, starting transfers between devices, move(): return lax.ppermute(value, axes if len(axes) > 1 else axes[0], pairs)  21.7 us
    ppermute x13, waiting for transfers between devices, move(): return lax.ppermute(value, axes if len(axes) > 1 else axes[0], pairs)  4.24 us
    pallas_call x1, Pallas kernels, pack(): pl.pallas_call(functools.partial(pack_kernel, held_count=held_count), out...  2.12 us
    pallas_call x2, Pallas kernels, expert_quarter(): pl.pallas_call(functools.partial(expert_kernel, count=len(blocks)), out_s...  1.48 us
    pallas_call x1, Pallas kernels, mix(): pl.pallas_call(functools.partial(mix_kernel, held_count=held_count), out_...  1.07 us
  transfers between devices with their start and end apart: 13, of which 3 were waited for; matrix products, arithmetic and copies ran while one was open for 0% of the time, Pallas kernels for 5%

profile of v5, /device:TPU:0, one launch (start us, length us, event | category | flops | bytes accessed | tf_op | source)
XLA Modules:
  0.0 30.8 jit_solution(5991628462572638289)
XLA Ops:
  0.0 2.1 %shard_map.64 = (bf16[8,128]{1,0:T(8,128)(2,1)S(1)}, bf16[24,1024]{1,0:T(8,128)(2,1)S(1)}, bf16[24,1024]{1,0:T(8,128)(2,1)S(1)}, bf16[2,2048,256]{2,1,0:T(8,128)(2,1)S(1)}, bf16[256,2048]{1,0:T(8,128)(2,1)S(1)}) custom-call(s32[1]{0:T(128)} %bitcast.base_ref, s32[8,128]{1,0:T(8,128)} %bitcast.14, f32[8,128]{1,0:T(8,128)} %bitcast.15, ...), custom_call_target="tpu_custom_call" | custom-call | tf_op jit(solution)/shard_map/pallas_call | solution.py:117
  2.1 5.1 %collective-permute-start.5 = (bf16[24,1024]{1,0:T(8,128)(2,1)S(1)}, bf16[24,1024]{1,0:T(8,128)(2,1)S(1)}, u32[]{:S(2)}, u32[]{:S(2)}) collective-permute-start(bf16[24,1024]{1,0:T(8,128)(2,1)S(1)} %get-tuple-element.16.refs_0_), channel_id=1, source_target_pairs={{0,6},{2,4},{4,2},{6,0},{1,7},{3,5},{5,3},{7,1},{8,14},{10,12},{12... | collective-permute-start | bytes 147464 | tf_op jit(solution)/shard_map/ppermute | solution.py:245
  7.2 0.0 collective-permute-start.3
  7.2 1.8 %collective-permute-start.6 = (bf16[24,1024]{1,0:T(8,128)(2,1)S(1)}, bf16[24,1024]{1,0:T(8,128)(2,1)S(1)}, u32[]{:S(2)}, u32[]{:S(2)}) collective-permute-start(bf16[24,1024]{1,0:T(8,128)(2,1)S(1)} %get-tuple-element.17), channel_id=1, source_target_pairs={{0,7},{1,6},{2,5},{3,4},{4,3},{5,2},{6,1},{7,0},{8,15},{9,14},{10,... | collective-permute-start | bytes 147464 | tf_op jit(solution)/shard_map/ppermute | solution.py:245
  9.1 1.1 %collective-permute-start.4 = (bf16[24,1024]{1,0:T(8,128)(2,1)S(1)}, bf16[24,1024]{1,0:T(8,128)(2,1)S(1)}, u32[]{:S(2)}, u32[]{:S(2)}) collective-permute-start(bf16[24,1024]{1,0:T(8,128)(2,1)S(1)} %get-tuple-element.17), channel_id=1, source_target_pairs={{0,3},{1,2},{2,1},{3,0},{4,7},{5,6},{6,5},{7,4},{8,11},{9,10},{10,... | collective-permute-start | bytes 147464 | tf_op jit(solution)/shard_map/ppermute | solution.py:245
  10.2 2.3 %collective-permute-start.1 = (bf16[24,1024]{1,0:T(8,128)(2,1)S(1)}, bf16[24,1024]{1,0:T(8,128)(2,1)S(1)}, u32[]{:S(2)}, u32[]{:S(2)}) collective-permute-start(bf16[24,1024]{1,0:T(8,128)(2,1)S(1)} %get-tuple-element.16.refs_0_), channel_id=1, source_target_pairs={{0,4},{2,6},{4,0},{6,2},{1,5},{3,7},{5,1},{7,3},{8,12},{10,14},{12... | collective-permute-start | bytes 147464 | tf_op jit(solution)/shard_map/ppermute | solution.py:245
  12.5 0.0 collective-permute-done.5.refs_2_
  12.5 0.9 %collective-permute-start.2 = (bf16[24,1024]{1,0:T(8,128)(2,1)S(1)}, bf16[24,1024]{1,0:T(8,128)(2,1)S(1)}, u32[]{:S(2)}, u32[]{:S(2)}) collective-permute-start(bf16[24,1024]{1,0:T(8,128)(2,1)S(1)} %get-tuple-element.17), channel_id=1, source_target_pairs={{0,5},{1,4},{2,7},{3,6},{4,1},{5,0},{6,3},{7,2},{8,13},{9,12},{10,... | collective-permute-start | bytes 147464 | tf_op jit(solution)/shard_map/ppermute | solution.py:245
  13.5 0.0 collective-permute-done.3.refs_0_
  13.5 1.1 %collective-permute-start = (bf16[24,1024]{1,0:T(8,128)(2,1)S(1)}, bf16[24,1024]{1,0:T(8,128)(2,1)S(1)}, u32[]{:S(2)}, u32[]{:S(2)}) collective-permute-start(bf16[24,1024]{1,0:T(8,128)(2,1)S(1)} %get-tuple-element.17), channel_id=1, source_target_pairs={{0,1},{1,0},{2,3},{3,2},{4,5},{5,4},{6,7},{7,6},{8,9},{9,8},{10,11... | collective-permute-start | bytes 147464 | tf_op jit(solution)/shard_map/ppermute | solution.py:245
  14.6 0.0 collective-permute-done.6.refs_3_
  14.6 0.2 collective-permute-done.4.refs_1_
  14.8 0.7 %shard_map.66 = (bf16[48,1024]{1,0:T(8,128)(2,1)S(1)}, bf16[48,1024]{1,0:T(8,128)(2,1)S(1)}) custom-call(bf16[2,2048,256]{2,1,0:T(8,128)(2,1)S(1)} %get-tuple-element.14.gate_up_ref, bf16[256,2048]{1,0:T(8,128)(2,1)S(1)} %get-tuple-element.15.down_ref, bf16[24,1024]{1,0:T(8,128)(2,1)S(1)} %collective-permute-done.3.refs_0_, ...), custom_call_target="tpu_custom_call" | custom-call | flops 1 | bytes 1 | tf_op jit(solution)/shard_map/pallas_call | solution.py:156
  15.6 0.9 %collective-permute-start.7 = (bf16[48,1024]{1,0:T(8,128)(2,1)S(1)}, bf16[48,1024]{1,0:T(8,128)(2,1)S(1)}, u32[]{:S(2)}, u32[]{:S(2)}) collective-permute-start(bf16[48,1024]{1,0:T(8,128)(2,1)S(1)} %get-tuple-element.19), channel_id=1, source_target_pairs={{0,2},{2,0},{4,6},{6,4},{1,3},{3,1},{5,7},{7,5},{8,10},{10,8},{12,... | collective-permute-start | bytes 294920 | tf_op jit(solution)/shard_map/ppermute | solution.py:245
  16.5 2.9 %collective-permute-start.8 = (bf16[48,1024]{1,0:T(8,128)(2,1)S(1)}, bf16[48,1024]{1,0:T(8,128)(2,1)S(1)}, u32[]{:S(2)}, u32[]{:S(2)}) collective-permute-start(bf16[48,1024]{1,0:T(8,128)(2,1)S(1)} %get-tuple-element.20), channel_id=1, source_target_pairs={{0,6},{2,4},{4,2},{6,0},{1,7},{3,5},{5,3},{7,1},{8,14},{10,12},{12... | collective-permute-start | bytes 294920 | tf_op jit(solution)/shard_map/ppermute | solution.py:245
  19.4 0.0 collective-permute-done.1.refs_2_
  19.4 0.0 collective-permute-done.2.refs_3_
  19.4 0.0 collective-permute-done.refs_1_
  19.4 0.7 %shard_map.65 = (bf16[48,1024]{1,0:T(8,128)(2,1)S(1)}, bf16[48,1024]{1,0:T(8,128)(2,1)S(1)}) custom-call(bf16[2,2048,256]{2,1,0:T(8,128)(2,1)S(1)} %get-tuple-element.14.gate_up_ref, bf16[256,2048]{1,0:T(8,128)(2,1)S(1)} %get-tuple-element.15.down_ref, bf16[24,1024]{1,0:T(8,128)(2,1)S(1)} %get-tuple-element.16.refs_0_, ...), custom_call_target="tpu_custom_call" | custom-call | flops 1 | bytes 1 | tf_op jit(solution)/shard_map/pallas_call | solution.py:156
  20.2 0.1 collective-permute-start.12
  20.2 4.5 %collective-permute-start.10 = (bf16[24,1024]{1,0:T(8,128)(2,1)S(1)}, bf16[24,1024]{1,0:T(8,128)(2,1)S(1)}, u32[]{:S(2)}, u32[]{:S(2)}) collective-permute-start(bf16[24,1024]{1,0:T(8,128)(2,1)S(1)} %get-tuple-element.26), channel_id=1, source_target_pairs={{0,12},{2,14},{4,8},{6,10},{8,20},{10,22},{12,16},{14,18},{16,28},... | collective-permute-start | bytes 147464 | tf_op jit(solution)/shard_map/ppermute | solution.py:245
  24.7 0.0 collective-permute-done.7
  24.7 0.0 collective-permute-done.8
  24.8 0.1 collective-permute-start.11
  24.9 0.8 %collective-permute-start.9 = (bf16[32,1024]{1,0:T(8,128)(2,1)S(1)}, bf16[32,1024]{1,0:T(8,128)(2,1)S(1)}, u32[]{:S(2)}, u32[]{:S(2)}) collective-permute-start(bf16[32,1024]{1,0:T(8,128)(2,1)S(1)} %fusion.1), channel_id=1, source_target_pairs={{0,8},{8,16},{16,24},{24,0},{1,9},{9,17},{17,25},{25,1},{2,10},{10... | collective-permute-start | bytes 196616 | tf_op jit(solution)/shard_map/ppermute | solution.py:245
  25.7 1.9 %collective-permute-done.12 = bf16[24,1024]{1,0:T(8,128)(2,1)S(1)} collective-permute-done((bf16[24,1024]{1,0:T(8,128)(2,1)S(1)}, bf16[24,1024]{1,0:T(8,128)(2,1)S(1)}, u32[]{:S(2)}, u32[]{:S(2)}) %collective-permute-start.12) | collective-permute-done | bytes 49184 | tf_op jit(solution)/shard_map/ppermute | solution.py:245
  27.6 2.1 %collective-permute-done.11 = bf16[24,1024]{1,0:T(8,128)(2,1)S(1)} collective-permute-done((bf16[24,1024]{1,0:T(8,128)(2,1)S(1)}, bf16[24,1024]{1,0:T(8,128)(2,1)S(1)}, u32[]{:S(2)}, u32[]{:S(2)}) %collective-permute-start.11) | collective-permute-done | bytes 49184 | tf_op jit(solution)/shard_map/ppermute | solution.py:245
  29.7 0.0 collective-permute-done.9
  29.7 0.0 collective-permute-done.10
  29.8 1.1 %shard_map.67 = bf16[128,2048]{1,0:T(8,128)(2,1)} custom-call(bf16[8,1024]{1,0:T(8,128)(2,1)S(1)} %slice.25.meta_ref, bf16[24,1024]{1,0:T(8,128)(2,1)S(1)} %add_convert_fusion.2.refs_0_, bf16[24,1024]{1,0:T(8,128)(2,1)S(1)} %add_convert_fusion.1.refs_1_), custom_call_target="tpu_custom_call" | custom-call | tf_op jit(solution)/shard_map/pallas_call | solution.py:220
  (7 shorter events, 0.1 us)
Async XLA Ops:
  2.1 10.4 %collective-permute-start.5 = (bf16[24,1024]{1,0:T(8,128)(2,1)S(1)}, bf16[24,1024]{1,0:T(8,128)(2,1)S(1)}, u32[]{:S(2)}, u32[]{:S(2)}) collective-permute-start(bf16[24,1024]{1,0:T(8,128)(2,1)S(1)} %get-tuple-element.16.refs_0_), channel_id=1, source_target_pairs={{0,6},{2,4},{4,2},{6,0},{1,7},{3,5},{5,3},{7,1},{8,14},{10,12},{12... | collective-permute-start | bytes 147464 | tf_op jit(solution)/shard_map/ppermute | solution.py:245
  7.2 6.2 %collective-permute-start.3 = (bf16[24,1024]{1,0:T(8,128)(2,1)S(1)}, bf16[24,1024]{1,0:T(8,128)(2,1)S(1)}, u32[]{:S(2)}, u32[]{:S(2)}) collective-permute-start(bf16[24,1024]{1,0:T(8,128)(2,1)S(1)} %get-tuple-element.16.refs_0_), channel_id=1, source_target_pairs={{0,2},{2,0},{4,6},{6,4},{1,3},{3,1},{5,7},{7,5},{8,10},{10,8},{12,... | collective-permute-start | bytes 147464 | tf_op jit(solution)/shard_map/ppermute | solution.py:245
  7.2 7.4 %collective-permute-start.6 = (bf16[24,1024]{1,0:T(8,128)(2,1)S(1)}, bf16[24,1024]{1,0:T(8,128)(2,1)S(1)}, u32[]{:S(2)}, u32[]{:S(2)}) collective-permute-start(bf16[24,1024]{1,0:T(8,128)(2,1)S(1)} %get-tuple-element.17), channel_id=1, source_target_pairs={{0,7},{1,6},{2,5},{3,4},{4,3},{5,2},{6,1},{7,0},{8,15},{9,14},{10,... | collective-permute-start | bytes 147464 | tf_op jit(solution)/shard_map/ppermute | solution.py:245
  9.1 5.8 %collective-permute-start.4 = (bf16[24,1024]{1,0:T(8,128)(2,1)S(1)}, bf16[24,1024]{1,0:T(8,128)(2,1)S(1)}, u32[]{:S(2)}, u32[]{:S(2)}) collective-permute-start(bf16[24,1024]{1,0:T(8,128)(2,1)S(1)} %get-tuple-element.17), channel_id=1, source_target_pairs={{0,3},{1,2},{2,1},{3,0},{4,7},{5,6},{6,5},{7,4},{8,11},{9,10},{10,... | collective-permute-start | bytes 147464 | tf_op jit(solution)/shard_map/ppermute | solution.py:245
  10.2 9.2 %collective-permute-start.1 = (bf16[24,1024]{1,0:T(8,128)(2,1)S(1)}, bf16[24,1024]{1,0:T(8,128)(2,1)S(1)}, u32[]{:S(2)}, u32[]{:S(2)}) collective-permute-start(bf16[24,1024]{1,0:T(8,128)(2,1)S(1)} %get-tuple-element.16.refs_0_), channel_id=1, source_target_pairs={{0,4},{2,6},{4,0},{6,2},{1,5},{3,7},{5,1},{7,3},{8,12},{10,14},{12... | collective-permute-start | bytes 147464 | tf_op jit(solution)/shard_map/ppermute | solution.py:245
  12.5 6.8 %collective-permute-start.2 = (bf16[24,1024]{1,0:T(8,128)(2,1)S(1)}, bf16[24,1024]{1,0:T(8,128)(2,1)S(1)}, u32[]{:S(2)}, u32[]{:S(2)}) collective-permute-start(bf16[24,1024]{1,0:T(8,128)(2,1)S(1)} %get-tuple-element.17), channel_id=1, source_target_pairs={{0,5},{1,4},{2,7},{3,6},{4,1},{5,0},{6,3},{7,2},{8,13},{9,12},{10,... | collective-permute-start | bytes 147464 | tf_op jit(solution)/shard_map/ppermute | solution.py:245
  13.5 5.9 %collective-permute-start = (bf16[24,1024]{1,0:T(8,128)(2,1)S(1)}, bf16[24,1024]{1,0:T(8,128)(2,1)S(1)}, u32[]{:S(2)}, u32[]{:S(2)}) collective-permute-start(bf16[24,1024]{1,0:T(8,128)(2,1)S(1)} %get-tuple-element.17), channel_id=1, source_target_pairs={{0,1},{1,0},{2,3},{3,2},{4,5},{5,4},{6,7},{7,6},{8,9},{9,8},{10,11... | collective-permute-start | bytes 147464 | tf_op jit(solution)/shard_map/ppermute | solution.py:245
  15.6 9.2 %collective-permute-start.7 = (bf16[48,1024]{1,0:T(8,128)(2,1)S(1)}, bf16[48,1024]{1,0:T(8,128)(2,1)S(1)}, u32[]{:S(2)}, u32[]{:S(2)}) collective-permute-start(bf16[48,1024]{1,0:T(8,128)(2,1)S(1)} %get-tuple-element.19), channel_id=1, source_target_pairs={{0,2},{2,0},{4,6},{6,4},{1,3},{3,1},{5,7},{7,5},{8,10},{10,8},{12,... | collective-permute-start | bytes 294920 | tf_op jit(solution)/shard_map/ppermute | solution.py:245
  16.5 8.2 %collective-permute-start.8 = (bf16[48,1024]{1,0:T(8,128)(2,1)S(1)}, bf16[48,1024]{1,0:T(8,128)(2,1)S(1)}, u32[]{:S(2)}, u32[]{:S(2)}) collective-permute-start(bf16[48,1024]{1,0:T(8,128)(2,1)S(1)} %get-tuple-element.20), channel_id=1, source_target_pairs={{0,6},{2,4},{4,2},{6,0},{1,7},{3,5},{5,3},{7,1},{8,14},{10,12},{12... | collective-permute-start | bytes 294920 | tf_op jit(solution)/shard_map/ppermute | solution.py:245
  20.2 7.4 %collective-permute-start.12 = (bf16[24,1024]{1,0:T(8,128)(2,1)S(1)}, bf16[24,1024]{1,0:T(8,128)(2,1)S(1)}, u32[]{:S(2)}, u32[]{:S(2)}) collective-permute-start(bf16[24,1024]{1,0:T(8,128)(2,1)S(1)} %get-tuple-element.25), channel_id=1, source_target_pairs={{0,13},{1,12},{2,15},{3,14},{4,9},{5,8},{6,11},{7,10},{8,21},{9,20... | collective-permute-start | bytes 147464 | tf_op jit(solution)/shard_map/ppermute | solution.py:245
  20.2 9.5 %collective-permute-start.10 = (bf16[24,1024]{1,0:T(8,128)(2,1)S(1)}, bf16[24,1024]{1,0:T(8,128)(2,1)S(1)}, u32[]{:S(2)}, u32[]{:S(2)}) collective-permute-start(bf16[24,1024]{1,0:T(8,128)(2,1)S(1)} %get-tuple-element.26), channel_id=1, source_target_pairs={{0,12},{2,14},{4,8},{6,10},{8,20},{10,22},{12,16},{14,18},{16,28},... | collective-permute-start | bytes 147464 | tf_op jit(solution)/shard_map/ppermute | solution.py:245
  24.8 4.9 %collective-permute-start.11 = (bf16[24,1024]{1,0:T(8,128)(2,1)S(1)}, bf16[24,1024]{1,0:T(8,128)(2,1)S(1)}, u32[]{:S(2)}, u32[]{:S(2)}) collective-permute-start(bf16[24,1024]{1,0:T(8,128)(2,1)S(1)} %get-tuple-element.23), channel_id=1, source_target_pairs={{0,9},{1,8},{8,17},{9,16},{16,25},{17,24},{24,1},{25,0},{2,11},{3,... | collective-permute-start | bytes 147464 | tf_op jit(solution)/shard_map/ppermute | solution.py:245
  24.9 4.8 %collective-permute-start.9 = (bf16[32,1024]{1,0:T(8,128)(2,1)S(1)}, bf16[32,1024]{1,0:T(8,128)(2,1)S(1)}, u32[]{:S(2)}, u32[]{:S(2)}) collective-permute-start(bf16[32,1024]{1,0:T(8,128)(2,1)S(1)} %fusion.1), channel_id=1, source_target_pairs={{0,8},{8,16},{16,24},{24,0},{1,9},{9,17},{17,25},{25,1},{2,10},{10... | collective-permute-start | bytes 196616 | tf_op jit(solution)/shard_map/ppermute | solution.py:245
